TPU v7x, 256 devices: a whole 4x4x8 slice. The times are simulated.
256 devices in a mesh: shot: 2 (over z_lo), gx: 32 (over x, z_hi, core), gy: 4 (over y).
Axes of the slice: x: 4, y: 4, z: 8 (z_hi: 4, z_lo: 2; z = z_hi * 2 + z_lo), core: 2. Of those that a mesh axis runs over, the one named last changes fastest.
Arguments:
- velocity: float32 [256, 32, 256], P('gx', 'gy', 'shot'), may hold values from 0.2 to 0.42
- density: float32 [256, 32, 256], P('gx', 'gy', 'shot'), may hold values from 1 to 4
- stored_fields: float32 [1024, 2, 16, 256], P('gx', None, ('shot', 'gy')), may hold values from -6 to 6
- holders: int32 [32, 32], P('gx'), may hold values from 0 to 31, each once within a row
- adjoint_init: float32 [2, 2, 256, 32, 256], P('shot', None, 'gx', 'gy'), may hold values from -6 to 6
- traces: float32 [2, 4, 256, 32], P('shot', None, 'gx', 'gy'), may hold values from -24 to 24
- aperture: int32 [2, 2], replicated, may hold values from 0 to 32, as said below
Outputs:
- image: float32 [256, 32, 256], P('gx', 'gy', 'shot')
- forward_end: float32 [2, 2, 256, 32, 256], P('shot', None, 'gx', 'gy')
- adjoint_end: float32 [2, 2, 256, 32, 256], P('shot', None, 'gx', 'gy')
Inputs may be any that keep to these rules, and one draw needn't show every extreme that they name: Each row of holders is a permutation of 0 to 31. aperture[s, 0] < aperture[s, 1] for every shot.
All inputs are finite; a program needn't handle non-finite values.
Results may differ from a plain program's by a relative error of at most 0.00002.
Values sent between devices are 32-bit elements; how exact they have to be, the bound alone decides.
A program may use at most 192 MiB of HBM per device.

v0:
```python
import jax
import jax.numpy as jnp
from jax import lax
from jax.sharding import PartitionSpec as P

REC_Z = 8


LAPLACE_TAPS = (-205.0 / 72.0, 8.0 / 5.0, -1.0 / 5.0, 8.0 / 315.0, -1.0 / 560.0)
SLOPE_TAPS = (4.0 / 5.0, -1.0 / 5.0, 4.0 / 105.0, -1.0 / 280.0)


def padded(cells, sides, width):
    for axis, dim in sides:
        count = lax.axis_size(axis)
        ends = count - 1
        head = lax.slice_in_dim(cells, 0, width, axis=dim)
        tail = lax.slice_in_dim(cells, cells.shape[dim] - width, cells.shape[dim], axis=dim)
        cells = jnp.concatenate(
            [
                lax.ppermute(tail, axis, [(i, (i + 1) % count) for i in range(ends)]),
                cells,
                lax.ppermute(head, axis, [((i + 1) % count, i) for i in range(ends)]),
            ],
            axis=dim,
        )
    return cells


def window(extended, offsets):
    lengths = [extended.shape[extended.ndim - 3 + dimension] - 8 for dimension in range(3)]
    starts = [4 + offsets[dimension] for dimension in range(3)]
    return extended[
        ...,
        starts[0] : starts[0] + lengths[0],
        starts[1] : starts[1] + lengths[1],
        starts[2] : starts[2] + lengths[2],
    ]


def moved(spatial, amount):
    offsets = [0, 0, 0]
    offsets[spatial] = amount
    return tuple(offsets)


def laplace(extended):
    summed = 3.0 * LAPLACE_TAPS[0] * window(extended, (0, 0, 0))
    for radius in range(1, 5):
        paired = window(extended, moved(0, radius)) + window(extended, moved(0, -radius))
        for spatial in (1, 2):
            paired = (
                paired
                + window(extended, moved(spatial, radius))
                + window(extended, moved(spatial, -radius))
            )
        summed = summed + LAPLACE_TAPS[radius] * paired
    return summed


def slope(extended, spatial):
    summed = SLOPE_TAPS[0] * (
        window(extended, moved(spatial, 1)) - window(extended, moved(spatial, -1))
    )
    for radius in range(2, 5):
        summed = summed + SLOPE_TAPS[radius - 1] * (
            window(extended, moved(spatial, radius)) - window(extended, moved(spatial, -radius))
        )
    return summed


def advance(extended, previous, speed_sq, log_grads):
    advection = (
        log_grads[0] * slope(extended, 0)
        + log_grads[1] * slope(extended, 1)
        + log_grads[2] * slope(extended, 2)
    )
    return 2.0 * window(extended, (0, 0, 0)) - previous + speed_sq * (laplace(extended) - advection)


def pad_depth(field):
    widths = [(0, 0)] * (field.ndim - 1) + [(4, 4)]
    return jnp.pad(field, widths)


def shards(velocity, density, stored_fields, holders, adjoint_init, traces, aperture):
    speed_whole, density_whole = (
        lax.all_gather(velocity, "shot", axis=2, tiled=True),
        lax.all_gather(density, "shot", axis=2, tiled=True),
    )
    speed_sq = speed_whole * speed_whole
    log_density = jnp.log(density_whole)
    width_x, width_y, depth_cells = speed_sq.shape
    received = lax.all_to_all(stored_fields, "gx", split_axis=0, concat_axis=0, tiled=True)
    piece_order = jnp.argsort(holders[0])
    pieces = jnp.take(received, piece_order, axis=0)
    checkpoint = jnp.transpose(pieces, (1, 0, 2, 3)).reshape(2, width_x, width_y, depth_cells)
    current = jnp.stack([checkpoint[0], adjoint_init[0, 0]])
    previous = jnp.stack([checkpoint[1], adjoint_init[0, 1]])
    steps_total = traces.shape[1]
    forwards = {}
    backwards = {steps_total: adjoint_init[0, 0]}
    log_wide = padded(log_density, (("gx", 0), ("gy", 1)), 4)
    padded_log = pad_depth(log_wide)
    grads_core = [slope(padded_log, spatial) for spatial in range(3)]
    for number in range(1, steps_total + 1):
        extended = padded(current, (("gx", 1), ("gy", 2)), 4)
        advanced = advance(pad_depth(extended), previous, speed_sq, grads_core)
        advanced = advanced.at[1, :, :, REC_Z].add(
            speed_sq[:, :, REC_Z] * traces[0, steps_total - number]
        )
        previous, current = (current, advanced)
        forwards[number] = current[0]
        backwards[steps_total - number] = current[1]
    correlation = forwards[1] * backwards[1]
    for number in range(2, steps_total + 1):
        correlation = correlation + forwards[number] * backwards[number]
    shot_rows = jnp.arange(aperture.shape[0], dtype=jnp.int32)[:, None] == lax.axis_index("shot")
    bounds = jnp.sum(jnp.where(shot_rows, aperture, 0), axis=0)
    block_pos = lax.axis_index("gx")
    active = ((block_pos >= bounds[0]) & (block_pos < bounds[1])).astype(jnp.float32)
    image = lax.psum_scatter(active * correlation, "shot", scatter_dimension=2, tiled=True)
    forward_end = jnp.stack([forwards[steps_total], forwards[steps_total - 1]])[None]
    adjoint_end = jnp.stack([backwards[0], backwards[1]])[None]
    return (image, forward_end, adjoint_end)


def solution(mesh):
    return jax.shard_map(
        shards,
        mesh=mesh,
        in_specs=(
            P("gx", "gy", "shot"),
            P("gx", "gy", "shot"),
            P("gx", None, ("shot", "gy"), None),
            P("gx", None),
            P("shot", None, "gx", "gy", None),
            P("shot", None, "gx", "gy"),
            P(),
        ),
        out_specs=(
            P("gx", "gy", "shot"),
            P("shot", None, "gx", "gy", None),
            P("shot", None, "gx", "gy", None),
        ),
        check_vma=False,
    )
```

profile of v0, /device:TPU:1, one launch (start us, length us, event | category | flops | bytes accessed | tf_op | source)
XLA Modules:
  0.0 719.2 jit_solution(13213368511273073689)
XLA Ops:
  7.2 12.6 %all-to-all-start = ((f32[32,2,2,256]{3,2,1,0:T(2,128)}), f32[32,2,2,256]{3,2,1,0:T(2,128)S(1)}, u32[]{:S(2)}, u32[]{:S(2)}) async-start(f32[32,2,2,256]{3,2,1,0:T(2,128)} %param.17), calls=%async_computation | async-start | bytes 262144 | tf_op jit(solution)/shard_map/all_to_all | solution.py:94
  19.8 4.8 all_gather.7
  27.4 4.0 collective-permute-start.5
  35.2 3.6 all_gather.6
  43.2 4.0 collective-permute-start.7
  52.8 3.9 collective-permute-start.1
  59.4 3.6 copy.310
  63.6 4.8 collective-permute-start.3
  71.7 3.0 copy.327
  88.5 8.1 %add_multiply_fusion.2 = f32[2,8,8,256]{2,1,3,0:T(8,128)} fusion(f32[2,8,8,256]{2,1,3,0:T(8,128)} %copy.333, f32[2,8,8,256]{2,1,3,0:T(8,128)} %copy.334, f32[2,8,8,256]{2,1,3,0:T(8,128)} %copy.331, f32[2,8,8,256]{2,1,3,0:T(8,128)} %copy.332, f32[2,8,8,256]{2,1,3,0:T(8,128)} %copy.329, f32[2,8,8,256]{2,1,3,0:T(8,128)} %copy.330, f32[2,8,8,256]{2,1,3,0:T(8,128)} %copy.327, ...), kind=kLoop, calls=%fused_computation.26 | loop fusion | flops 393216 | bytes 1245184 | tf_op jit(solution)/shard_map/mul | solution.py:74
  104.6 2.9 copy.338
  121.6 8.1 %add_multiply_fusion.1 = f32[2,8,8,256]{2,1,3,0:T(8,128)} fusion(f32[2,8,8,256]{2,1,3,0:T(8,128)} %copy.342, f32[2,8,8,256]{2,1,3,0:T(8,128)} %copy.343, f32[2,8,8,256]{2,1,3,0:T(8,128)} %copy.340, f32[2,8,8,256]{2,1,3,0:T(8,128)} %copy.341, f32[2,8,8,256]{2,1,3,0:T(8,128)} %copy.338, f32[2,8,8,256]{2,1,3,0:T(8,128)} %copy.339, f32[2,8,8,256]{2,1,3,0:T(8,128)} %copy.336, ...), kind=kLoop, calls=%fused_computation.25 | loop fusion | flops 393216 | bytes 1245184 | tf_op jit(solution)/shard_map/mul | solution.py:75
  138.0 4.4 copy.309
  142.4 4.4 copy.311
  146.8 5.8 select_maximum_fusion.12
  152.6 10.3 %add_multiply_fusion.6 = (f32[2,8,8,256]{2,1,3,0:T(8,128)}, f32[2,8,8,256]{2,1,3,0:T(8,128)}, f32[2,8,8,256]{2,1,3,0:T(8,128)}, f32[2,8,8,256]{2,1,3,0:T(8,128)}) fusion(f32[2,8,8,256]{2,1,3,0:T(8,128)} %copy.312, f32[2,16,16,264]{2,1,3,0:T(8,128)S(1)} %select_maximum_fusion.12, f32[2,8,8,256]{2,1,3,0:T(8,128)} %copy.316, f32[2,8,8,256]{2,1,3,0:T(8,128)} %copy.320, ...), kind=kLoop, calls=%fused_computation.30 | loop fusion | flops 688128 | bytes 2031616 | tf_op jit(solution)/shard_map/mul | solution.py:57
  165.7 3.0 copy.317
  173.6 5.9 add_multiply_fusion.3
  194.3 4.2 collective-permute-start.9
  217.2 4.8 fusion.133
  222.0 3.6 copy.361
  225.6 4.2 copy.362
  229.8 4.3 collective-permute-start.11
  234.1 4.2 copy.360
  242.3 2.9 copy.376
  248.1 2.9 copy.378
  298.4 3.7 copy.364
  302.1 4.4 copy.365
  306.5 7.5 %select_maximum_fusion.8 = f32[2,16,16,264]{2,1,3,0:T(8,128)} fusion(f32[2,16,4,256]{2,1,3,0:T(8,128)} %copy.365, f32[2,16,4,256]{2,1,3,0:T(8,128)} %copy.364, f32[2,4,8,256]{2,1,3,0:T(4,128)} %copy.359, f32[2,8,8,256]{2,1,3,0:T(8,128)S(1)} %fusion.112, f32[2,4,8,256]{2,1,3,0:T(4,128)} %copy.358), kind=kLoop, calls=%fused_computation.11 | loop fusion | flops 1622016 | bytes 1064960 | tf_op jit(solution)/shard_map/concatenate | solution.py:19
  314.0 30.5 %multiply_add_fusion.2 = f32[2,8,8,256]{2,1,3,0:T(8,128)} fusion(f32[2,8,8,256]{2,1,3,0:T(8,128)} %copy.392, f32[2,8,8,256]{2,1,3,0:T(8,128)} %copy.390, f32[2,8,8,256]{2,1,3,0:T(8,128)} %copy.391, f32[2,8,8,256]{2,1,3,0:T(8,128)} %copy.388, f32[2,8,8,256]{2,1,3,0:T(8,128)} %copy.389, f32[2,8,8,256]{2,1,3,0:T(8,128)} %copy.386, f32[2,8,8,256]{2,1,3,0:T(8,128)} %copy.387, ...), kind=kLoop, calls=%fused_computation.23 | loop fusion | flops 1900544 | bytes 4325376 | tf_op jit(solution)/shard_map/add | solution.py:78
  345.7 3.9 fusion.137
  351.1 4.8 collective-permute-start.13
  366.8 3.1 pad_maximum_fusion.1
  372.0 4.8 fusion.132
  376.8 3.6 copy.402
  380.5 4.2 copy.403
  384.6 4.3 collective-permute-start.15
  388.9 4.6 copy.401
  399.9 2.9 copy.418
  405.7 2.9 copy.420
  439.5 2.9 copy.425
  453.2 3.7 copy.405
  456.9 4.4 copy.406
  461.3 7.8 %select_maximum_fusion.4 = f32[2,16,16,264]{2,1,3,0:T(8,128)} fusion(f32[2,16,4,256]{2,1,3,0:T(8,128)} %copy.406, f32[2,16,4,256]{2,1,3,0:T(8,128)} %copy.405, f32[2,4,8,256]{2,1,3,0:T(4,128)} %copy.400, f32[2,8,8,256]{2,1,3,0:T(8,128)} %fusion.111, f32[2,4,8,256]{2,1,3,0:T(4,128)} %copy.399), kind=kLoop, calls=%fused_computation.7 | loop fusion | flops 1622016 | bytes 1064960 | tf_op jit(solution)/shard_map/concatenate | solution.py:19
  469.1 30.6 %multiply_add_fusion.1 = f32[2,8,8,256]{2,1,3,0:T(8,128)} fusion(f32[2,8,8,256]{2,1,3,0:T(8,128)} %copy.431, f32[2,8,8,256]{2,1,3,0:T(8,128)} %copy.432, f32[2,8,8,256]{2,1,3,0:T(8,128)} %copy.429, f32[2,8,8,256]{2,1,3,0:T(8,128)} %copy.430, f32[2,8,8,256]{2,1,3,0:T(8,128)} %copy.427, f32[2,8,8,256]{2,1,3,0:T(8,128)} %copy.428, f32[2,8,8,256]{2,1,3,0:T(8,128)} %copy.425, ...), kind=kLoop, calls=%fused_computation.22 | loop fusion | flops 1966080 | bytes 4325376 | tf_op jit(solution)/shard_map/add | solution.py:78
  501.0 3.9 fusion.136
  506.4 4.8 collective-permute-start.17
  514.7 3.0 fusion.135
  527.4 3.1 pad_maximum_fusion.2
  532.6 4.8 fusion.131
  537.4 3.6 copy.442
  541.1 4.2 copy.443
  545.2 4.3 collective-permute-start.19
  549.5 4.2 copy.441
  560.4 2.9 copy.458
  566.1 2.9 copy.460
  599.9 2.9 copy.465
  613.6 3.8 copy.445
  617.4 4.4 copy.446
  621.8 7.8 %select_maximum_fusion = f32[2,16,16,264]{2,1,3,0:T(8,128)} fusion(f32[2,16,4,256]{2,1,3,0:T(8,128)} %copy.446, f32[2,16,4,256]{2,1,3,0:T(8,128)} %copy.445, f32[2,4,8,256]{2,1,3,0:T(4,128)} %copy.440, f32[2,8,8,256]{2,1,3,0:T(8,128)} %fusion.110, f32[2,4,8,256]{2,1,3,0:T(4,128)} %copy.439), kind=kLoop, calls=%fused_computation.3 | loop fusion | flops 1622016 | bytes 1064960 | tf_op jit(solution)/shard_map/concatenate | solution.py:19
  629.6 31.0 %multiply_add_fusion = f32[2,8,8,256]{2,1,3,0:T(8,128)} fusion(f32[2,8,8,256]{2,1,3,0:T(8,128)} %copy.471, f32[2,8,8,256]{2,1,3,0:T(8,128)} %copy.472, f32[2,8,8,256]{2,1,3,0:T(8,128)} %copy.469, f32[2,8,8,256]{2,1,3,0:T(8,128)} %copy.470, f32[2,8,8,256]{2,1,3,0:T(8,128)} %copy.467, f32[2,8,8,256]{2,1,3,0:T(8,128)} %copy.468, f32[2,8,8,256]{2,1,3,0:T(8,128)} %copy.465, ...), kind=kLoop, calls=%fused_computation.21 | loop fusion | flops 1966080 | bytes 4325376 | tf_op jit(solution)/shard_map/add | solution.py:78
  661.9 3.0 fusion.134
  666.5 3.9 fusion.4
  673.3 36.8 %reduce-scatter.2.cloned.1.call-done = f32[8,8,128]{1,0,2:T(8,128)} async-done(((f32[8,8,256]{1,0,2:T(8,128)}), f32[8,8,128]{1,0,2:T(8,128)}) %reduce-scatter.2.cloned.1.call-update) | async-done | bytes 32784 | tf_op jit(solution)/shard_map/reduce_scatter | solution.py:122
  (300 shorter events, 304.4 us)
Async XLA Ops:
  7.2 42.1 %all-to-all-start = ((f32[32,2,2,256]{3,2,1,0:T(2,128)}), f32[32,2,2,256]{3,2,1,0:T(2,128)S(1)}, u32[]{:S(2)}, u32[]{:S(2)}) async-start(f32[32,2,2,256]{3,2,1,0:T(2,128)} %param.17), calls=%async_computation | async-start | bytes 262144 | tf_op jit(solution)/shard_map/all_to_all | solution.py:94
  19.8 690.4 %reduce-scatter.2.cloned.1.call-start = ((), (), s32[]{:S(2)}) async-start(), calls=%async_computation.2 | async-start | bytes 1572864 | tf_op jit(solution)/shard_map/reduce_scatter | solution.py:122
  24.7 17.2 %collective-permute-start.4 = (f32[4,8,256]{2,1,0:T(8,128)S(1)}, f32[4,8,256]{2,1,0:T(8,128)S(1)}, u32[]{:S(2)}, u32[]{:S(2)}) collective-permute-start(f32[4,8,256]{2,1,0:T(8,128)S(1)} %get-tuple-element.222), channel_id=1, source_target_pairs={{4,0},{8,4},{12,8},{16,12},{20,16},{24,20},{28,24},{32,28},{36,32}... | collective-permute-start | bytes 98312 | tf_op jit(solution)/shard_map/ppermute | solution.py:23
  27.4 14.5 %collective-permute-start.5 = (f32[4,8,256]{2,1,0:T(8,128)S(1)}, f32[4,8,256]{2,1,0:T(8,128)S(1)}, u32[]{:S(2)}, u32[]{:S(2)}) collective-permute-start(f32[4,8,256]{2,1,0:T(8,128)S(1)} %get-tuple-element.221), channel_id=1, source_target_pairs={{0,4},{4,8},{8,12},{12,16},{16,20},{20,24},{24,28},{28,32},{32,36}... | collective-permute-start | bytes 98312 | tf_op jit(solution)/shard_map/ppermute | solution.py:21
  41.5 7.7 %copy-start.5 = (f32[1,1,8,8,256]{3,2,4,1,0:T(8,128)}, f32[1,1,8,8,256]{3,2,4,1,0:T(8,128)S(1)}, u32[]{:S(2)}) copy-start(f32[1,1,8,8,256]{3,2,4,1,0:T(8,128)S(1)} %copy.478) | copy-start | bytes 196612
  41.9 6.0 collective-permute-start.6
  43.2 5.6 collective-permute-start.7
  50.2 9.1 %collective-permute-start = (f32[2,4,8,256]{3,2,1,0:T(8,128)S(1)}, f32[2,4,8,256]{3,2,1,0:T(8,128)S(1)}, u32[]{:S(2)}, u32[]{:S(2)}) collective-permute-start(f32[2,4,8,256]{3,2,1,0:T(8,128)S(1)} %get-tuple-element.216), channel_id=1, source_target_pairs={{4,0},{8,4},{12,8},{16,12},{20,16},{24,20},{28,24},{32,28},{36,32}... | collective-permute-start | bytes 196616 | tf_op jit(solution)/shard_map/ppermute | solution.py:23
  52.8 6.5 collective-permute-start.1
  57.3 64.3 %copy-start.4 = (f32[8,8,256]{1,0,2:T(8,128)}, f32[8,8,256]{1,0,2:T(8,128)S(1)}, u32[]{:S(2)}) copy-start(f32[8,8,256]{1,0,2:T(8,128)S(1)} %copy.335) | copy-start | bytes 196612
  63.6 35.8 %collective-permute-start.3 = (f32[2,16,4,256]{3,1,2,0:T(8,128)}, f32[2,16,4,256]{3,1,2,0:T(8,128)}, u32[]{:S(2)}, u32[]{:S(2)}) collective-permute-start(f32[2,16,4,256]{3,1,2,0:T(8,128)} %copy.579), channel_id=1, source_target_pairs={{0,1},{1,2},{2,3},{4,5},{5,6},{6,7},{8,9},{9,10},{10,11},{12,13},{... | collective-permute-start | bytes 393224 | tf_op jit(solution)/shard_map/ppermute | solution.py:21
  69.1 31.4 %collective-permute-start.2 = (f32[2,16,4,256]{3,1,2,0:T(8,128)}, f32[2,16,4,256]{3,1,2,0:T(8,128)}, u32[]{:S(2)}, u32[]{:S(2)}) collective-permute-start(f32[2,16,4,256]{3,1,2,0:T(8,128)} %copy.578), channel_id=1, source_target_pairs={{1,0},{2,1},{3,2},{5,4},{6,5},{7,6},{9,8},{10,9},{11,10},{13,12},{... | collective-permute-start | bytes 393224 | tf_op jit(solution)/shard_map/ppermute | solution.py:23
  71.7 5.0 copy-start.10
  71.7 6.9 copy-start.9
  71.7 10.9 %copy-start.8 = (f32[2,8,8,256]{3,2,1,0:T(8,128)}, f32[2,8,8,256]{3,2,1,0:T(8,128)S(1)}, u32[]{:S(2)}) copy-start(f32[2,8,8,256]{3,2,1,0:T(8,128)S(1)} %get-tuple-element.189) | copy-start | bytes 393220
  76.6 4.0 copy-start.11
  80.6 4.0 copy-start.12
  104.6 2.9 copy-start.23
  104.6 5.0 copy-start.18
  107.5 4.1 copy-start.42
  152.6 10.3 %copy-start = (f32[2,16,16,264]{2,1,3,0:T(8,128)}, f32[2,16,16,264]{2,1,3,0:T(8,128)S(1)}, u32[]{:S(2)}) copy-start(f32[2,16,16,264]{2,1,3,0:T(8,128)S(1)} %select_maximum_fusion.12) | copy-start | bytes 1622020
  165.7 5.8 copy-start.7
  168.7 4.2 copy-start.16
  179.6 2.3 copy-start.24
  179.6 2.3 copy-start.28
  179.6 2.3 copy-start.32
  179.6 2.3 copy-start.47
  179.6 2.3 copy-start.48
  194.3 13.9 %collective-permute-start.9 = (f32[2,4,8,256]{3,2,1,0:T(8,128)}, f32[2,4,8,256]{3,2,1,0:T(8,128)}, u32[]{:S(2)}, u32[]{:S(2)}) collective-permute-start(f32[2,4,8,256]{3,2,1,0:T(8,128)} %copy.354), channel_id=1, source_target_pairs={{0,4},{4,8},{8,12},{12,16},{16,20},{20,24},{24,28},{28,32},{32,36}... | collective-permute-start | bytes 196616 | tf_op jit(solution)/shard_map/ppermute | solution.py:21
  200.7 9.7 %collective-permute-start.8 = (f32[2,4,8,256]{3,2,1,0:T(8,128)}, f32[2,4,8,256]{3,2,1,0:T(8,128)}, u32[]{:S(2)}, u32[]{:S(2)}) collective-permute-start(f32[2,4,8,256]{3,2,1,0:T(8,128)} %copy.352), channel_id=1, source_target_pairs={{4,0},{8,4},{12,8},{16,12},{20,16},{24,20},{28,24},{32,28},{36,32}... | collective-permute-start | bytes 196616 | tf_op jit(solution)/shard_map/ppermute | solution.py:23
  229.8 35.4 %collective-permute-start.11 = (f32[2,16,4,256]{3,1,2,0:T(8,128)}, f32[2,16,4,256]{3,1,2,0:T(8,128)S(1)}, u32[]{:S(2)}, u32[]{:S(2)}) collective-permute-start(f32[2,16,4,256]{3,1,2,0:T(8,128)} %copy.362), channel_id=1, source_target_pairs={{0,1},{1,2},{2,3},{4,5},{5,6},{6,7},{8,9},{9,10},{10,11},{12,13},{... | collective-permute-start | bytes 393224 | tf_op jit(solution)/shard_map/ppermute | solution.py:21
  238.3 26.9 %collective-permute-start.10 = (f32[2,16,4,256]{3,1,2,0:T(8,128)}, f32[2,16,4,256]{3,1,2,0:T(8,128)}, u32[]{:S(2)}, u32[]{:S(2)}) collective-permute-start(f32[2,16,4,256]{3,1,2,0:T(8,128)} %copy.360), channel_id=1, source_target_pairs={{1,0},{2,1},{3,2},{5,4},{6,5},{7,6},{9,8},{10,9},{11,10},{13,12},{... | collective-permute-start | bytes 393224 | tf_op jit(solution)/shard_map/ppermute | solution.py:23
  278.0 2.9 copy-start.39
  278.0 4.9 copy-start.36
  282.8 4.9 copy-start.33
  284.9 4.8 copy-start.29
  289.6 4.8 copy-start.25
  291.6 4.8 copy-start.20
  351.1 13.0 %collective-permute-start.13 = (f32[2,4,8,256]{3,2,1,0:T(8,128)S(1)}, f32[2,4,8,256]{3,2,1,0:T(8,128)S(1)}, u32[]{:S(2)}, u32[]{:S(2)}) collective-permute-start(f32[2,4,8,256]{3,2,1,0:T(8,128)S(1)} %copy.395), channel_id=1, source_target_pairs={{0,4},{4,8},{8,12},{12,16},{16,20},{20,24},{24,28},{28,32},{32,36}... | collective-permute-start | bytes 196616 | tf_op jit(solution)/shard_map/ppermute | solution.py:21
  357.5 8.0 %collective-permute-start.12 = (f32[2,4,8,256]{3,2,1,0:T(8,128)S(1)}, f32[2,4,8,256]{3,2,1,0:T(8,128)S(1)}, u32[]{:S(2)}, u32[]{:S(2)}) collective-permute-start(f32[2,4,8,256]{3,2,1,0:T(8,128)S(1)} %copy.393), channel_id=1, source_target_pairs={{4,0},{8,4},{12,8},{16,12},{20,16},{24,20},{28,24},{32,28},{36,32}... | collective-permute-start | bytes 196616 | tf_op jit(solution)/shard_map/ppermute | solution.py:23
  364.1 5.8 copy-start.43
  365.5 4.4 copy-start.44
  384.6 35.4 %collective-permute-start.15 = (f32[2,16,4,256]{3,1,2,0:T(8,128)}, f32[2,16,4,256]{3,1,2,0:T(8,128)S(1)}, u32[]{:S(2)}, u32[]{:S(2)}) collective-permute-start(f32[2,16,4,256]{3,1,2,0:T(8,128)} %copy.403), channel_id=1, source_target_pairs={{0,1},{1,2},{2,3},{4,5},{5,6},{6,7},{8,9},{9,10},{10,11},{12,13},{... | collective-permute-start | bytes 393224 | tf_op jit(solution)/shard_map/ppermute | solution.py:21
  393.5 26.5 %collective-permute-start.14 = (f32[2,16,4,256]{3,1,2,0:T(8,128)}, f32[2,16,4,256]{3,1,2,0:T(8,128)}, u32[]{:S(2)}, u32[]{:S(2)}) collective-permute-start(f32[2,16,4,256]{3,1,2,0:T(8,128)} %copy.401), channel_id=1, source_target_pairs={{1,0},{2,1},{3,2},{5,4},{6,5},{7,6},{9,8},{10,9},{11,10},{13,12},{... | collective-permute-start | bytes 393224 | tf_op jit(solution)/shard_map/ppermute | solution.py:23
  432.8 2.9 copy-start.40
  432.8 4.8 copy-start.37
  437.6 4.8 copy-start.34
  439.5 4.9 copy-start.30
  444.5 4.8 copy-start.26
  446.4 4.8 copy-start.21
  506.4 18.4 %collective-permute-start.17 = (f32[2,4,8,256]{3,2,1,0:T(8,128)S(1)}, f32[2,4,8,256]{3,2,1,0:T(8,128)S(1)}, u32[]{:S(2)}, u32[]{:S(2)}) collective-permute-start(f32[2,4,8,256]{3,2,1,0:T(8,128)S(1)} %copy.435), channel_id=1, source_target_pairs={{0,4},{4,8},{8,12},{12,16},{16,20},{20,24},{24,28},{28,32},{32,36}... | collective-permute-start | bytes 196616 | tf_op jit(solution)/shard_map/ppermute | solution.py:21
  512.7 13.3 %collective-permute-start.16 = (f32[2,4,8,256]{3,2,1,0:T(8,128)S(1)}, f32[2,4,8,256]{3,2,1,0:T(8,128)S(1)}, u32[]{:S(2)}, u32[]{:S(2)}) collective-permute-start(f32[2,4,8,256]{3,2,1,0:T(8,128)S(1)} %copy.433), channel_id=1, source_target_pairs={{4,0},{8,4},{12,8},{16,12},{20,16},{24,20},{28,24},{32,28},{36,32}... | collective-permute-start | bytes 196616 | tf_op jit(solution)/shard_map/ppermute | solution.py:23
  524.7 5.8 copy-start.45
  526.1 4.4 copy-start.46
  545.2 35.2 %collective-permute-start.19 = (f32[2,16,4,256]{3,1,2,0:T(8,128)}, f32[2,16,4,256]{3,1,2,0:T(8,128)S(1)}, u32[]{:S(2)}, u32[]{:S(2)}) collective-permute-start(f32[2,16,4,256]{3,1,2,0:T(8,128)} %copy.443), channel_id=1, source_target_pairs={{0,1},{1,2},{2,3},{4,5},{5,6},{6,7},{8,9},{9,10},{10,11},{12,13},{... | collective-permute-start | bytes 393224 | tf_op jit(solution)/shard_map/ppermute | solution.py:21
  553.7 26.8 %collective-permute-start.18 = (f32[2,16,4,256]{3,1,2,0:T(8,128)}, f32[2,16,4,256]{3,1,2,0:T(8,128)}, u32[]{:S(2)}, u32[]{:S(2)}) collective-permute-start(f32[2,16,4,256]{3,1,2,0:T(8,128)} %copy.441), channel_id=1, source_target_pairs={{1,0},{2,1},{3,2},{5,4},{6,5},{7,6},{9,8},{10,9},{11,10},{13,12},{... | collective-permute-start | bytes 393224 | tf_op jit(solution)/shard_map/ppermute | solution.py:23
  593.2 2.9 copy-start.41
  593.2 4.8 copy-start.38
  598.0 4.8 copy-start.35
  599.9 4.9 copy-start.31
  604.9 4.8 copy-start.27
  606.8 4.8 copy-start.22
  661.9 4.6 copy-start.6
  666.5 3.9 copy-start.50
  (9 other events, 19.8 us)
Sparse Core Ops, SparseCore 0:
  670.5 39.5 reduce-scatter.1
where the time goes:
time: 726 us; the launch traced here: 719 us
  local copies, waits for them, and re-layouts  379 us (52%)
  other arithmetic  202 us (28%)
  starting transfers between devices  74.7 us (10%)
  waiting for transfers between devices  38 us (5%)
  between operations  16.6 us (2%)
  blocking collectives  8.45 us (1%)
    slice x67, local copies, waits for them, and re-layouts, window(): extended[..., starts[0]:starts[0] + lengths[0], starts[1]:starts[1] + len...  162 us
    add x4, other arithmetic, advance(): 2.0 * window(extended, (0, 0, 0)) - previous  94.5 us
    concatenate x15, other arithmetic, padded(): jnp.concatenate([lax.ppermute(tail, axis, [(i, (i + 1) % count) for i in...  45.1 us
    ppermute x10, starting transfers between devices, padded(): lax.ppermute(tail, axis, [(i, (i + 1) % count) for i in range(ends)])  43.2 us
    slice x12, local copies, waits for them, and re-layouts, padded(): head = lax.slice_in_dim(cells, 0, width, axis=dim)  42 us
    reduce_scatter x1, waiting for transfers between devices, shards(): lax.psum_scatter(active * correlation, 'shot', scatter_dimension=2, tiled...  36.8 us
    add x16, local copies, waits for them, and re-layouts, laplace(): paired + window(extended, moved(spatial, radius))  35.7 us
    ppermute x7, local copies, waits for them, and re-layouts, padded(): lax.ppermute(head, axis, [((i + 1) % count, i) for i in range(ends)])  22.4 us
  transfers between devices with their start and end apart: 22, of which 3 were waited for; matrix products, arithmetic and copies ran while one was open for 22% of the time, Pallas kernels for 0%

commit v1 on v0

v1 whole, which is shorter than its diff:
```python
import functools

import jax
import jax.numpy as jnp
from jax import lax
from jax.experimental import pallas as pl
from jax.experimental.pallas import tpu as pltpu
from jax.sharding import PartitionSpec as P

REC_Z = 8
STEPS = 4
LAPLACE_TAPS = (-205.0 / 72.0, 8.0 / 5.0, -1.0 / 5.0, 8.0 / 315.0, -1.0 / 560.0)
SLOPE_TAPS = (4.0 / 5.0, -1.0 / 5.0, 4.0 / 105.0, -1.0 / 280.0)


def y_plus(centre, halo, row, k):
    return pltpu.roll(jnp.where(row < k, halo, centre), 8 - k, 1)


def y_minus(centre, halo, row, k):
    return pltpu.roll(jnp.where(row >= 8 - k, halo, centre), k, 1)


def z_plus(lower, upper, lane, k):
    low, up = pltpu.roll(lower, 128 - k, 2), pltpu.roll(upper, 128 - k, 2)
    return jnp.where(lane < 128 - k, low, up), up


def z_minus(lower, upper, lane, k):
    low, up = pltpu.roll(lower, k, 2), pltpu.roll(upper, k, 2)
    return low, jnp.where(lane >= k, up, low)


def kernel(
    n_x,
    n_y,
    velocity,
    density,
    stored,
    holders,
    adjoint,
    traces,
    aperture,
    image_out,
    forward_out,
    adjoint_out,
    field,
    halo,
    before,
    last,
    coef,
    dens,
    dens_y,
    speed,
    pieces,
    holders_v,
    traces_v,
    aperture_v,
    inject,
    share,
    partner_share,
    image_v,
    small_sem,
    local_sem,
    own_sem,
    piece_sem,
    model_sem,
    send_sem,
    halo_send,
    halo_recv,
    image_sem,
    out_sem,
):
    s, b, j = lax.axis_index("shot"), lax.axis_index("gx"), lax.axis_index("gy")
    other = 1 - s
    right, left = lax.rem(b + 1, n_x), lax.rem(b + n_x - 1, n_x)
    up, down = lax.rem(j + 1, n_y), lax.rem(j + n_y - 1, n_y)

    smalls = [
        pltpu.make_async_copy(holders, holders_v, small_sem.at[0]),
        pltpu.make_async_copy(traces.at[0], traces_v, small_sem.at[1]),
        pltpu.make_async_copy(aperture, aperture_v, small_sem.at[2]),
    ]
    owns = [
        pltpu.make_async_copy(adjoint.at[0, 0], field.at[1, 0, pl.ds(4, 8)], own_sem.at[0]),
        pltpu.make_async_copy(adjoint.at[0, 1], before.at[1], own_sem.at[1]),
    ]
    own_model = [
        pltpu.make_async_copy(density, dens.at[s, pl.ds(4, 8)], local_sem.at[0]),
        pltpu.make_async_copy(velocity, speed.at[s], local_sem.at[1]),
        pltpu.make_async_copy(stored.at[b], pieces.at[b], local_sem.at[2]),
    ]
    for copy in smalls + owns + own_model:
        copy.start()

    barrier = pltpu.get_barrier_semaphore()

    def greet(step, carry):
        pl.semaphore_signal(barrier, inc=1, device_id={"gx": lax.rem(b + step, n_x)})
        return carry

    lax.fori_loop(1, n_x, greet, 0)
    near = [
        {"shot": other},
        {"shot": other, "gx": right},
        {"shot": other, "gx": left},
        {"gy": up},
        {"gy": down},
        {"shot": other, "gy": up},
        {"shot": other, "gy": down},
    ]
    for target in near:
        pl.semaphore_signal(barrier, inc=1, device_id=target)
    pl.semaphore_wait(barrier, n_x - 1 + len(near))

    def send_piece(step, carry):
        target = lax.rem(b + step, n_x)
        pltpu.make_async_remote_copy(
            stored.at[target], pieces.at[b], send_sem.at[0], piece_sem, device_id={"gx": target}
        ).start()
        return carry

    lax.fori_loop(1, n_x, send_piece, 0)

    def halo_sends(which, level, source):
        edges = [
            (source(pl.ds(4, 4), None), field.at[which, level, pl.ds(0, 4)], {"gx": right}),
            (source(pl.ds(0, 4), None), field.at[which, level, pl.ds(12, 4)], {"gx": left}),
            (source(pl.ds(0, 8), pl.ds(0, 4)), halo.at[which, level, :, pl.ds(0, 4)], {"gy": down}),
            (source(pl.ds(0, 8), pl.ds(4, 4)), halo.at[which, level, :, pl.ds(4, 4)], {"gy": up}),
        ]
        copies = []
        for side, (src, dst, target) in enumerate(edges):
            copies.append(
                pltpu.make_async_remote_copy(
                    src,
                    dst,
                    halo_send.at[which, level, side],
                    halo_recv.at[which, level, side],
                    device_id=target,
                )
            )
        for copy in copies:
            copy.start()
        return copies

    def from_argument(planes, rows):
        return adjoint.at[0, 0, planes] if rows is None else adjoint.at[0, 0, planes, rows]

    def from_field(which, level):
        def source(planes, rows):
            planes = pl.ds(planes.start + 4, planes.size)
            if rows is None:
                return field.at[which, level, planes]
            return field.at[which, level, planes, rows]

        return source

    sends = {(1, 0): halo_sends(1, 0, from_argument)}

    model = [
        (velocity, speed.at[s], {"shot": other}),
        (density, dens.at[s, pl.ds(4, 8)], {"shot": other}),
    ]
    for place in (s, other):
        model += [
            (density.at[pl.ds(4, 4)], dens.at[s, pl.ds(0, 4)], {"shot": place, "gx": right}),
            (density.at[pl.ds(0, 4)], dens.at[s, pl.ds(12, 4)], {"shot": place, "gx": left}),
            (density.at[:, pl.ds(0, 4)], dens_y.at[s, :, pl.ds(0, 4)], {"shot": place, "gy": down}),
            (density.at[:, pl.ds(4, 4)], dens_y.at[s, :, pl.ds(4, 4)], {"shot": place, "gy": up}),
        ]
    model_copies = []
    for at, (src, dst, target) in enumerate(model):
        copy = pltpu.make_async_remote_copy(
            src, dst, send_sem.at[1 + at], model_sem.at[at], device_id=target
        )
        copy.start()
        model_copies.append(copy)

    row = lax.broadcasted_iota(jnp.int32, (8, 8, 128), 1)
    lane = lax.broadcasted_iota(jnp.int32, (8, 8, 128), 2)
    low, high = pl.ds(0, 128), pl.ds(128, 128)

    for copy in smalls:
        copy.wait()
    column = lax.broadcasted_iota(jnp.int32, (64, n_x), 0)
    place = column // 2
    parity = column - 2 * place
    hit = holders_v[...] == place
    picks = [jnp.where(hit & (parity == r), 1.0, 0.0).astype(jnp.float32) for r in range(2)]

    bounds = aperture_v[...]
    bounds = jnp.where(s == 0, bounds[0:1], bounds[1:2])
    active = jnp.where((b >= bounds[:, 0:1]) & (b < bounds[:, 1:2]), 1.0, 0.0).astype(jnp.float32)
    active = active.reshape(1, 1, 1)

    for copy in own_model[:2]:
        copy.wait()
    for copy in model_copies:
        copy.wait_recv()

    first_x, last_x = b == 0, b == n_x - 1
    first_y, last_y = j == 0, j == n_y - 1
    keep_left = jnp.where(first_x, 0.0, 1.0).astype(jnp.float32)
    keep_right = jnp.where(last_x, 0.0, 1.0).astype(jnp.float32)
    keep_down = jnp.where(first_y, 0.0, 1.0).astype(jnp.float32)
    keep_up = jnp.where(last_y, 0.0, 1.0).astype(jnp.float32)
    logs, logs_y = [], []
    for half in range(2):
        wide = jnp.log(dens[half])
        logs.append(
            jnp.concatenate([wide[:4] * keep_left, wide[4:12], wide[12:] * keep_right], axis=0)
        )
        logs_y.append(jnp.log(dens_y[half]) * jnp.where(row < 4, keep_up, keep_down))
    inner = [logs[half][4:12] for half in range(2)]
    grad_x, grad_y, grad_z = [0.0, 0.0], [0.0, 0.0], [0.0, 0.0]
    for k in range(1, 5):
        tap = SLOPE_TAPS[k - 1]
        ahead = z_plus(inner[0], inner[1], lane, k)
        behind = z_minus(inner[0], inner[1], lane, k)
        ahead = (ahead[0], jnp.where(lane < 128 - k, ahead[1], 0.0))
        behind = (jnp.where(lane >= k, behind[0], 0.0), behind[1])
        for half in range(2):
            wide = logs[half]
            grad_x[half] += tap * (wide[4 + k : 12 + k] - wide[4 - k : 12 - k])
            grad_y[half] += tap * (
                y_plus(inner[half], logs_y[half], row, k)
                - y_minus(inner[half], logs_y[half], row, k)
            )
            grad_z[half] += tap * (ahead[half] - behind[half])

    for half, lanes in enumerate((low, high)):
        root = speed[half]
        sq = root * root
        coef[0, :, :, lanes] = 2.0 + (3.0 * LAPLACE_TAPS[0]) * sq
        for k in range(1, 5):
            even = LAPLACE_TAPS[k] * sq
            at = 1 + 6 * (k - 1)
            odd = SLOPE_TAPS[k - 1] * (sq * grad_x[half])
            plus, minus = even - odd, even + odd
            coef[at, : 8 - k, :, lanes] = plus[: 8 - k]
            coef[at, 8 - k :, :, lanes] = plus[8 - k :] * keep_right
            coef[at + 1, :k, :, lanes] = minus[:k] * keep_left
            coef[at + 1, k:, :, lanes] = minus[k:]
            odd = SLOPE_TAPS[k - 1] * (sq * grad_y[half])
            coef[at + 2, :, :, lanes] = (even - odd) * jnp.where(row >= 8 - k, keep_up, 1.0)
            coef[at + 3, :, :, lanes] = (even + odd) * jnp.where(row < k, keep_down, 1.0)
            odd = SLOPE_TAPS[k - 1] * (sq * grad_z[half])
            plus, minus = even - odd, even + odd
            if half == 0:
                minus = jnp.where(lane >= k, minus, 0.0)
            else:
                plus = jnp.where(lane < 128 - k, plus, 0.0)
            coef[at + 4, :, :, lanes] = plus
            coef[at + 5, :, :, lanes] = minus
        if half == 0:
            eye = lax.broadcasted_iota(jnp.int32, (8, 8), 0) == lax.broadcasted_iota(
                jnp.int32, (8, 8), 1
            )
            at_receiver = lax.broadcasted_iota(jnp.int32, (8, 128), 1) == REC_Z
            for number in range(STEPS):
                for x in range(8):
                    line = jnp.where(eye, traces_v[number, pl.ds(x, 1), :], 0.0)
                    line = jnp.sum(line, axis=1, keepdims=True)
                    inject[number, x] = jnp.where(at_receiver, line, 0.0) * sq[x]

    def advance(which, level):
        previous = before.at[which] if level == 0 else field.at[which, level - 1, pl.ds(4, 8)]
        wide = field.at[which, level]
        centre = [wide[4:12, :, lanes] for lanes in (low, high)]
        edge = [halo[which, level, :, :, lanes] for lanes in (low, high)]
        total = [
            coef[0, :, :, lanes] * centre[half] - previous[:, :, lanes]
            for half, lanes in enumerate((low, high))
        ]
        for k in range(1, 5):
            at = 1 + 6 * (k - 1)
            ahead = z_plus(centre[0], centre[1], lane, k)
            behind = z_minus(centre[0], centre[1], lane, k)
            for half, lanes in enumerate((low, high)):
                total[half] = (
                    total[half]
                    + coef[at, :, :, lanes] * wide[4 + k : 12 + k, :, lanes]
                    + coef[at + 1, :, :, lanes] * wide[4 - k : 12 - k, :, lanes]
                    + coef[at + 2, :, :, lanes] * y_plus(centre[half], edge[half], row, k)
                    + coef[at + 3, :, :, lanes] * y_minus(centre[half], edge[half], row, k)
                    + coef[at + 4, :, :, lanes] * ahead[half]
                    + coef[at + 5, :, :, lanes] * behind[half]
                )
        if which == 1:
            total[0] = total[0] + inject[STEPS - 1 - level]
        return total

    def step(which, level):
        for copy in sends[which, level]:
            copy.wait_recv()
        new = advance(which, level)
        if level == STEPS - 1:
            for half, lanes in enumerate((low, high)):
                last[which, :, :, lanes] = new[half]
            return
        for half, lanes in enumerate((low, high)):
            field[which, level + 1, 4:12, :, lanes] = new[half]
        sends[which, level + 1] = halo_sends(which, level + 1, from_field(which, level + 1))

    for copy in owns:
        copy.wait()
    step(1, 0)

    own_model[2].wait()
    pltpu.make_async_copy(pieces.at[pl.ds(0, n_x - 1)], pieces.at[pl.ds(0, n_x - 1)], piece_sem).wait()
    for level in (0, 1):
        found = 0.0
        for r in range(2):
            found += jnp.dot(
                picks[r],
                pieces[:, level, r, :],
                precision=lax.Precision.HIGHEST,
                preferred_element_type=jnp.float32,
            )
        found = found.reshape(8, 8, 256)
        if level == 0:
            field[0, 0, 4:12] = found
            sends[0, 0] = halo_sends(0, 0, from_field(0, 0))
        else:
            before[0] = found

    step(1, 1)
    step(0, 0)
    step(1, 2)
    outs = [
        pltpu.make_async_copy(field.at[1, 3, pl.ds(4, 8)], adjoint_out.at[0, 1], out_sem.at[0])
    ]
    outs[0].start()
    step(0, 1)
    step(1, 3)
    outs.append(pltpu.make_async_copy(last.at[1], adjoint_out.at[0, 0], out_sem.at[1]))
    outs[1].start()
    step(0, 2)
    outs.append(
        pltpu.make_async_copy(field.at[0, 3, pl.ds(4, 8)], forward_out.at[0, 1], out_sem.at[2])
    )
    outs[2].start()
    early = [0.0, 0.0]
    for number in range(1, STEPS):
        for half, lanes in enumerate((low, high)):
            early[half] += (
                field[0, number, 4:12, :, lanes] * field[1, STEPS - number, 4:12, :, lanes]
            )
    step(0, 3)
    outs.append(pltpu.make_async_copy(last.at[0], forward_out.at[0, 0], out_sem.at[3]))
    outs[3].start()
    whole = [
        active * (early[half] + last[0, :, :, lanes] * field[1, 0, 4:12, :, lanes])
        for half, lanes in enumerate((low, high))
    ]
    share[...] = jnp.where(s == 0, whole[1], whole[0])
    to_partner = pltpu.make_async_remote_copy(
        share, partner_share, image_sem.at[0], image_sem.at[1], device_id={"shot": other}
    )
    to_partner.start()
    mine = jnp.where(s == 0, whole[0], whole[1])

    pltpu.make_async_copy(
        stored.at[pl.ds(0, n_x - 1)], stored.at[pl.ds(0, n_x - 1)], send_sem.at[0]
    ).wait()
    for copy in model_copies:
        copy.wait_send()
    for copies in sends.values():
        for copy in copies:
            copy.wait_send()

    to_partner.wait()
    image_v[...] = mine + partner_share[...]
    outs.append(pltpu.make_async_copy(image_v, image_out, out_sem.at[4]))
    outs[4].start()
    for copy in outs:
        copy.wait()


def shards(n_x, n_y, velocity, density, stored, holders, adjoint, traces, aperture):
    f32 = jnp.float32
    anywhere = pl.BlockSpec(memory_space=pl.ANY)
    return pl.pallas_call(
        functools.partial(kernel, n_x, n_y),
        out_shape=(
            jax.ShapeDtypeStruct((8, 8, 128), f32),
            jax.ShapeDtypeStruct((1, 2, 8, 8, 256), f32),
            jax.ShapeDtypeStruct((1, 2, 8, 8, 256), f32),
        ),
        in_specs=[anywhere] * 7,
        out_specs=(anywhere,) * 3,
        scratch_shapes=[
            pltpu.VMEM((2, STEPS, 16, 8, 256), f32),
            pltpu.VMEM((2, STEPS, 8, 8, 256), f32),
            pltpu.VMEM((2, 8, 8, 256), f32),
            pltpu.VMEM((2, 8, 8, 256), f32),
            pltpu.VMEM((25, 8, 8, 256), f32),
            pltpu.VMEM((2, 16, 8, 128), f32),
            pltpu.VMEM((2, 8, 8, 128), f32),
            pltpu.VMEM((2, 8, 8, 128), f32),
            pltpu.VMEM((n_x, 2, 2, 256), f32),
            pltpu.VMEM((1, n_x), jnp.int32),
            pltpu.VMEM((STEPS, 8, 8), f32),
            pltpu.VMEM((2, 2), jnp.int32),
            pltpu.VMEM((STEPS, 8, 8, 128), f32),
            pltpu.VMEM((8, 8, 128), f32),
            pltpu.VMEM((8, 8, 128), f32),
            pltpu.VMEM((8, 8, 128), f32),
            pltpu.SemaphoreType.DMA((3,)),
            pltpu.SemaphoreType.DMA((3,)),
            pltpu.SemaphoreType.DMA((2,)),
            pltpu.SemaphoreType.DMA,
            pltpu.SemaphoreType.DMA((10,)),
            pltpu.SemaphoreType.DMA((11,)),
            pltpu.SemaphoreType.DMA((2, STEPS, 4)),
            pltpu.SemaphoreType.DMA((2, STEPS, 4)),
            pltpu.SemaphoreType.DMA((2,)),
            pltpu.SemaphoreType.DMA((5,)),
        ],
        compiler_params=pltpu.CompilerParams(
            collective_id=0, has_side_effects=True, vmem_limit_bytes=48 * 1024 * 1024
        ),
        cost_estimate=pl.CostEstimate(flops=8_000_000, bytes_accessed=800_000, transcendentals=0),
    )(velocity, density, stored, holders, adjoint, traces, aperture)


def solution(mesh):
    return jax.shard_map(
        functools.partial(shards, mesh.shape["gx"], mesh.shape["gy"]),
        mesh=mesh,
        in_specs=(
            P("gx", "gy", "shot"),
            P("gx", "gy", "shot"),
            P("gx", None, ("shot", "gy"), None),
            P("gx", None),
            P("shot", None, "gx", "gy", None),
            P("shot", None, "gx", "gy"),
            P(),
        ),
        out_specs=(
            P("gx", "gy", "shot"),
            P("shot", None, "gx", "gy", None),
            P("shot", None, "gx", "gy", None),
        ),
        check_vma=False,
    )
```

time: 726 us -> 53.9 us (0.07)
  the two profiles are of different devices: /device:TPU:1 before, /device:TPU:32 now
where the time goes in v1:
time: 53.9 us; the launch traced here: 53.6 us
  Pallas kernels  45.7 us (85%)
  local copies, waits for them, and re-layouts  7.29 us (14%)
  between operations  0.66 us (1%)
    pallas_call x1, Pallas kernels, shards(): pl.pallas_call(functools.partial(kernel, n_x, n_y), out_shape=(jax.ShapeD...  45.7 us
    unnamed x17, local copies, waits for them, and re-layouts  7.29 us

profile of v1, /device:TPU:32, one launch (start us, length us, event | category | flops | bytes accessed | tf_op | source)
XLA Modules:
  0.0 53.6 jit_solution(273570369854262600)
XLA Ops:
  0.6 0.0 copy-start
  0.6 0.9 %copy-done = f32[32,2,2,256]{3,2,1,0:T(2,128)S(1)} copy-done((f32[32,2,2,256]{3,2,1,0:T(2,128)S(1)}, f32[32,2,2,256]{3,2,1,0:T(2,128)}, u32[]{:S(2)}) %copy-start) | copy-done | bytes 131096
  1.5 0.0 copy-start.1
  1.5 0.9 %copy-done.1 = f32[1,2,8,8,256]{4,3,2,1,0:T(8,128)S(1)} copy-done((f32[1,2,8,8,256]{4,3,2,1,0:T(8,128)S(1)}, f32[1,2,8,8,256]{4,3,2,1,0:T(8,128)}, u32[]{:S(2)}) %copy-start.1) | copy-done | bytes 131096
  2.4 0.0 copy-start.2
  2.4 0.8 %copy-done.2 = f32[8,8,128]{2,1,0:T(8,128)S(1)} copy-done((f32[8,8,128]{2,1,0:T(8,128)S(1)}, f32[8,8,128]{2,1,0:T(8,128)}, u32[]{:S(2)}) %copy-start.2) | copy-done | bytes 32792
  3.2 0.0 copy-start.3
  3.2 0.8 %copy-done.3 = f32[8,8,128]{2,1,0:T(8,128)S(1)} copy-done((f32[8,8,128]{2,1,0:T(8,128)S(1)}, f32[8,8,128]{2,1,0:T(8,128)}, u32[]{:S(2)}) %copy-start.3) | copy-done | bytes 32792
  4.0 0.0 copy-start.4
  4.0 0.7 %copy-done.4 = f32[1,4,8,8]{3,2,1,0:T(8,128)S(1)} copy-done((f32[1,4,8,8]{3,2,1,0:T(8,128)S(1)}, f32[1,4,8,8]{3,2,1,0:T(8,128)}, u32[]{:S(2)}) %copy-start.4) | copy-done | bytes 1048
  4.7 0.0 copy-start.5
  4.7 0.7 %copy-done.5 = s32[2,2]{1,0:T(2,128)S(1)} copy-done((s32[2,2]{1,0:T(2,128)S(1)}, s32[2,2]{1,0:T(2,128)}, u32[]{:S(2)}) %copy-start.5) | copy-done | bytes 40
  5.4 0.0 copy-start.6
  5.4 0.7 %copy-done.6 = s32[1,32]{1,0:T(1,128)S(1)} copy-done((s32[1,32]{1,0:T(1,128)S(1)}, s32[1,32]{1,0:T(1,128)}, u32[]{:S(2)}) %copy-start.6) | copy-done | bytes 152
  6.0 45.7 %shard_map.94 = (f32[8,8,128]{2,1,0:T(8,128)S(1)}, f32[1,2,8,8,256]{4,3,2,1,0:T(8,128)S(1)}, f32[1,2,8,8,256]{4,3,2,1,0:T(8,128)S(1)}) custom-call(f32[8,8,128]{2,1,0:T(8,128)S(1)} %copy-done.2, f32[8,8,128]{2,1,0:T(8,128)S(1)} %copy-done.3, f32[32,2,2,256]{3,2,1,0:T(2,128)S(1)} %copy-done, s32[1,32]{1,0:T(1,128)S(1)} %copy-done.6, ...), custom_call_target="tpu_custom_call" | custom-call | flops 8000000 | bytes 800000 | tf_op jit(solution)/shard_map/pallas_call | solution.py:384
  51.7 0.6 %copy.13 = f32[8,8,128]{2,1,0:T(8,128)} copy(f32[8,8,128]{2,1,0:T(8,128)S(1)} %get-tuple-element.6) | data formatting | bytes 65536
  52.3 0.7 %copy.14 = f32[1,2,8,8,256]{4,3,2,1,0:T(8,128)} copy(f32[1,2,8,8,256]{4,3,2,1,0:T(8,128)S(1)} %get-tuple-element.7) | data formatting | bytes 262144
  53.0 0.7 %copy.15 = f32[1,2,8,8,256]{4,3,2,1,0:T(8,128)} copy(f32[1,2,8,8,256]{4,3,2,1,0:T(8,128)S(1)} %get-tuple-element.8) | data formatting | bytes 262144
Async XLA Ops:
  0.6 0.9 %copy-start = (f32[32,2,2,256]{3,2,1,0:T(2,128)S(1)}, f32[32,2,2,256]{3,2,1,0:T(2,128)}, u32[]{:S(2)}) copy-start(f32[32,2,2,256]{3,2,1,0:T(2,128)} %stored.1) | copy-start | bytes 393220
  1.5 0.9 %copy-start.1 = (f32[1,2,8,8,256]{4,3,2,1,0:T(8,128)S(1)}, f32[1,2,8,8,256]{4,3,2,1,0:T(8,128)}, u32[]{:S(2)}) copy-start(f32[1,2,8,8,256]{4,3,2,1,0:T(8,128)} %adjoint.1) | copy-start | bytes 393220
  2.4 0.8 %copy-start.2 = (f32[8,8,128]{2,1,0:T(8,128)S(1)}, f32[8,8,128]{2,1,0:T(8,128)}, u32[]{:S(2)}) copy-start(f32[8,8,128]{2,1,0:T(8,128)} %velocity.1) | copy-start | bytes 98308
  3.2 0.8 %copy-start.3 = (f32[8,8,128]{2,1,0:T(8,128)S(1)}, f32[8,8,128]{2,1,0:T(8,128)}, u32[]{:S(2)}) copy-start(f32[8,8,128]{2,1,0:T(8,128)} %density.1) | copy-start | bytes 98308
  4.0 0.7 %copy-start.4 = (f32[1,4,8,8]{3,2,1,0:T(8,128)S(1)}, f32[1,4,8,8]{3,2,1,0:T(8,128)}, u32[]{:S(2)}) copy-start(f32[1,4,8,8]{3,2,1,0:T(8,128)} %traces.1) | copy-start | bytes 3076
  4.7 0.7 %copy-start.5 = (s32[2,2]{1,0:T(2,128)S(1)}, s32[2,2]{1,0:T(2,128)}, u32[]{:S(2)}) copy-start(s32[2,2]{1,0:T(2,128)} %aperture.1) | copy-start | bytes 52
  5.4 0.7 %copy-start.6 = (s32[1,32]{1,0:T(1,128)S(1)}, s32[1,32]{1,0:T(1,128)}, u32[]{:S(2)}) copy-start(s32[1,32]{1,0:T(1,128)} %holders.1) | copy-start | bytes 388

commit v2 on v1

--- a/solution.py
+++ b/solution.py
@@ -59,7 +59,6 @@
     inject,
     share,
     partner_share,
-    image_v,
     small_sem,
     local_sem,
     own_sem,
@@ -93,6 +92,26 @@
     for copy in smalls + owns + own_model:
         copy.start()
 
+    @pl.when(b == 0)
+    def _():
+        field[:, :, :4] = jnp.zeros((2, STEPS, 4, 8, 256), jnp.float32)
+        dens[:, :4] = jnp.ones((2, 4, 8, 128), jnp.float32)
+
+    @pl.when(b == n_x - 1)
+    def _():
+        field[:, :, 12:] = jnp.zeros((2, STEPS, 4, 8, 256), jnp.float32)
+        dens[:, 12:] = jnp.ones((2, 4, 8, 128), jnp.float32)
+
+    @pl.when(j == 0)
+    def _():
+        halo[:, :, :, 4:] = jnp.zeros((2, STEPS, 8, 4, 256), jnp.float32)
+        dens_y[:, :, 4:] = jnp.ones((2, 8, 4, 128), jnp.float32)
+
+    @pl.when(j == n_y - 1)
+    def _():
+        halo[:, :, :, :4] = jnp.zeros((2, STEPS, 8, 4, 256), jnp.float32)
+        dens_y[:, :, :4] = jnp.ones((2, 8, 4, 128), jnp.float32)
+
     barrier = pltpu.get_barrier_semaphore()
 
     def greet(step, carry):
@@ -121,6 +140,23 @@
         return carry
 
     lax.fori_loop(1, n_x, send_piece, 0)
+
+    first_x, last_x = b == 0, b == n_x - 1
+    first_y, last_y = j == 0, j == n_y - 1
+    sends_to = [jnp.logical_not(edge) for edge in (last_x, first_x, first_y, last_y)]
+    gets_from = [jnp.logical_not(edge) for edge in (first_x, last_x, last_y, first_y)]
+
+    def start_all(copies, sides):
+        for copy, side in zip(copies, sides):
+            pl.when(sends_to[side])(copy.start)
+
+    def recv_all(copies, sides):
+        for copy, side in zip(copies, sides):
+            pl.when(gets_from[side])(copy.wait_recv)
+
+    def sent_all(copies, sides):
+        for copy, side in zip(copies, sides):
+            pl.when(sends_to[side])(copy.wait_send)
 
     def halo_sends(which, level, source):
         edges = [
@@ -140,8 +176,7 @@
                     device_id=target,
                 )
             )
-        for copy in copies:
-            copy.start()
+        start_all(copies, range(4))
         return copies
 
     def from_argument(planes, rows):
@@ -171,11 +206,14 @@
         ]
     model_copies = []
     for at, (src, dst, target) in enumerate(model):
-        copy = pltpu.make_async_remote_copy(
-            src, dst, send_sem.at[1 + at], model_sem.at[at], device_id=target
+        model_copies.append(
+            pltpu.make_async_remote_copy(
+                src, dst, send_sem.at[1 + at], model_sem.at[at], device_id=target
+            )
         )
+    for copy in model_copies[:2]:
         copy.start()
-        model_copies.append(copy)
+    start_all(model_copies[2:], (0, 1, 2, 3) * 2)
 
     row = lax.broadcasted_iota(jnp.int32, (8, 8, 128), 1)
     lane = lax.broadcasted_iota(jnp.int32, (8, 8, 128), 2)
@@ -196,11 +234,10 @@
 
     for copy in own_model[:2]:
         copy.wait()
-    for copy in model_copies:
+    for copy in model_copies[:2]:
         copy.wait_recv()
-
-    first_x, last_x = b == 0, b == n_x - 1
-    first_y, last_y = j == 0, j == n_y - 1
+    recv_all(model_copies[2:], (0, 1, 2, 3) * 2)
+
     keep_left = jnp.where(first_x, 0.0, 1.0).astype(jnp.float32)
     keep_right = jnp.where(last_x, 0.0, 1.0).astype(jnp.float32)
     keep_down = jnp.where(first_y, 0.0, 1.0).astype(jnp.float32)
@@ -292,8 +329,7 @@
         return total
 
     def step(which, level):
-        for copy in sends[which, level]:
-            copy.wait_recv()
+        recv_all(sends[which, level], range(4))
         new = advance(which, level)
         if level == STEPS - 1:
             for half, lanes in enumerate((low, high)):
@@ -364,32 +400,44 @@
     pltpu.make_async_copy(
         stored.at[pl.ds(0, n_x - 1)], stored.at[pl.ds(0, n_x - 1)], send_sem.at[0]
     ).wait()
-    for copy in model_copies:
+    for copy in model_copies[:2]:
         copy.wait_send()
+    sent_all(model_copies[2:], (0, 1, 2, 3) * 2)
     for copies in sends.values():
-        for copy in copies:
-            copy.wait_send()
+        sent_all(copies, range(4))
 
     to_partner.wait()
-    image_v[...] = mine + partner_share[...]
-    outs.append(pltpu.make_async_copy(image_v, image_out, out_sem.at[4]))
-    outs[4].start()
+    image_out[...] = mine + partner_share[...]
     for copy in outs:
+        copy.wait()
+
+
+def finish(image, forward, adjoint, image_out, forward_out, adjoint_out, sem):
+    copies = [
+        pltpu.make_async_copy(src, dst, sem.at[at])
+        for at, (src, dst) in enumerate(
+            ((image, image_out), (forward, forward_out), (adjoint, adjoint_out))
+        )
+    ]
+    for copy in copies:
+        copy.start()
+    for copy in copies:
         copy.wait()
 
 
 def shards(n_x, n_y, velocity, density, stored, holders, adjoint, traces, aperture):
     f32 = jnp.float32
     anywhere = pl.BlockSpec(memory_space=pl.ANY)
-    return pl.pallas_call(
+    inside = pl.BlockSpec(memory_space=pltpu.VMEM)
+    results = pl.pallas_call(
         functools.partial(kernel, n_x, n_y),
         out_shape=(
-            jax.ShapeDtypeStruct((8, 8, 128), f32),
-            jax.ShapeDtypeStruct((1, 2, 8, 8, 256), f32),
-            jax.ShapeDtypeStruct((1, 2, 8, 8, 256), f32),
+            pltpu.VMEM((8, 8, 128), f32),
+            pltpu.VMEM((1, 2, 8, 8, 256), f32),
+            pltpu.VMEM((1, 2, 8, 8, 256), f32),
         ),
         in_specs=[anywhere] * 7,
-        out_specs=(anywhere,) * 3,
+        out_specs=(inside,) * 3,
         scratch_shapes=[
             pltpu.VMEM((2, STEPS, 16, 8, 256), f32),
             pltpu.VMEM((2, STEPS, 8, 8, 256), f32),
@@ -406,7 +454,6 @@
             pltpu.VMEM((STEPS, 8, 8, 128), f32),
             pltpu.VMEM((8, 8, 128), f32),
             pltpu.VMEM((8, 8, 128), f32),
-            pltpu.VMEM((8, 8, 128), f32),
             pltpu.SemaphoreType.DMA((3,)),
             pltpu.SemaphoreType.DMA((3,)),
             pltpu.SemaphoreType.DMA((2,)),
@@ -416,13 +463,23 @@
             pltpu.SemaphoreType.DMA((2, STEPS, 4)),
             pltpu.SemaphoreType.DMA((2, STEPS, 4)),
             pltpu.SemaphoreType.DMA((2,)),
-            pltpu.SemaphoreType.DMA((5,)),
+            pltpu.SemaphoreType.DMA((4,)),
         ],
         compiler_params=pltpu.CompilerParams(
             collective_id=0, has_side_effects=True, vmem_limit_bytes=48 * 1024 * 1024
         ),
         cost_estimate=pl.CostEstimate(flops=8_000_000, bytes_accessed=800_000, transcendentals=0),
-    )(velocity, density, stored, holders, adjoint, traces, aperture)
+    )(*(
+        pltpu.with_memory_space_constraint(given, pltpu.HBM)
+        for given in (velocity, density, stored, holders, adjoint, traces, aperture)
+    ))
+    return pl.pallas_call(
+        finish,
+        out_shape=tuple(jax.ShapeDtypeStruct(one.shape, f32) for one in results),
+        in_specs=[inside] * 3,
+        out_specs=(anywhere,) * 3,
+        scratch_shapes=[pltpu.SemaphoreType.DMA((3,))],
+    )(*(pltpu.with_memory_space_constraint(one, pltpu.VMEM) for one in results))
 
 
 def solution(mesh):

time: 53.9 us -> 43.1 us (0.80)
  the two profiles are of different devices: /device:TPU:32 before, /device:TPU:18 now
where the time goes in v2:
time: 43.1 us; the launch traced here: 43 us
  Pallas kernels  42.3 us (98%)
  between operations  0.64 us (1%)
    pallas_call x1, Pallas kernels, shards(): pl.pallas_call(functools.partial(kernel, n_x, n_y), out_shape=(pltpu.VMEM...  41.6 us

profile of v2, /device:TPU:18, one launch (start us, length us, event | category | flops | bytes accessed | tf_op | source)
XLA Modules:
  0.0 43.0 jit_solution(2568903889099130797)
XLA Ops:
  0.6 41.6 %shard_map.94 = (f32[8,8,128]{2,1,0:T(8,128)S(1)}, f32[1,2,8,8,256]{4,3,2,1,0:T(8,128)S(1)}, f32[1,2,8,8,256]{4,3,2,1,0:T(8,128)S(1)}) custom-call(f32[8,8,128]{2,1,0:T(8,128)} %velocity.1, f32[8,8,128]{2,1,0:T(8,128)} %density.1, f32[32,2,2,256]{3,2,1,0:T(2,128)} %stored.1, s32[1,32]{1,0:T(1,128)} %holders.1, f32[1,2,8,8,256]{4,3,2,1,0:T(8,128)} %adjoint.1, ...), custom_call_target="tpu_custom_call" | custom-call | flops 8000000 | bytes 800000 | tf_op jit(solution)/shard_map/pallas_call | solution.py:432
  42.2 0.7 %shard_map.95 = (f32[8,8,128]{2,1,0:T(8,128)}, f32[1,2,8,8,256]{4,3,2,1,0:T(8,128)}, f32[1,2,8,8,256]{4,3,2,1,0:T(8,128)}) custom-call(f32[8,8,128]{2,1,0:T(8,128)S(1)} %get-tuple-element.6.image, f32[1,2,8,8,256]{4,3,2,1,0:T(8,128)S(1)} %get-tuple-element.7.forward, f32[1,2,8,8,256]{4,3,2,1,0:T(8,128)S(1)} %get-tuple-element.8.adjoint), custom_call_target="tpu_custom_call" | custom-call | tf_op jit(solution)/shard_map/pallas_call | solution.py:476

commit v3 on v2

v3 whole, which is shorter than its diff:
```python
import functools

import jax
import jax.numpy as jnp
from jax import lax
from jax.experimental import pallas as pl
from jax.experimental.pallas import tpu as pltpu
from jax.sharding import PartitionSpec as P

REC_Z = 8
STEPS = 4
LAPLACE_TAPS = (-205.0 / 72.0, 8.0 / 5.0, -1.0 / 5.0, 8.0 / 315.0, -1.0 / 560.0)
SLOPE_TAPS = (4.0 / 5.0, -1.0 / 5.0, 4.0 / 105.0, -1.0 / 280.0)


def y_plus(centre, halo, row, k):
    return pltpu.roll(jnp.where(row < k, halo, centre), 8 - k, 1)


def y_minus(centre, halo, row, k):
    return pltpu.roll(jnp.where(row >= 8 - k, halo, centre), k, 1)


def z_plus(lower, upper, lane, k):
    low, up = pltpu.roll(lower, 128 - k, 2), pltpu.roll(upper, 128 - k, 2)
    return jnp.where(lane < 128 - k, low, up), up


def z_minus(lower, upper, lane, k):
    low, up = pltpu.roll(lower, k, 2), pltpu.roll(upper, k, 2)
    return low, jnp.where(lane >= k, up, low)


def y_plus_outer(centre, above, below, row, k):
    return pltpu.roll(jnp.where(row < k, centre, jnp.where(row < k + 4, above, below)), 8 - k, 1)


def y_minus_outer(centre, above, below, row, k):
    return pltpu.roll(
        jnp.where(row >= 8 - k, centre, jnp.where(row < 4 - k, above, below)), k, 1
    )


def kernel(
    n_x,
    n_y,
    velocity,
    density,
    stored,
    holders,
    adjoint,
    traces,
    aperture,
    image_out,
    forward_out,
    adjoint_out,
    wide,
    below,
    above,
    corner,
    ring,
    mid,
    mid_y,
    old,
    old_y,
    back,
    back_y,
    back_old,
    last,
    coef,
    coef_y,
    dens,
    dens_below,
    dens_above,
    dens_corner,
    speed,
    speed_y,
    pieces,
    holders_v,
    traces_v,
    aperture_v,
    inject,
    share,
    partner_share,
    small_sem,
    local_sem,
    own_sem,
    piece_sem,
    piece_send,
    model_send,
    model_recv,
    deep_send,
    deep_recv,
    old_send,
    old_recv,
    back_send,
    back_recv,
    image_sem,
    out_sem,
):
    s, b, j = lax.axis_index("shot"), lax.axis_index("gx"), lax.axis_index("gy")
    other = 1 - s
    f32 = jnp.float32

    smalls = [
        pltpu.make_async_copy(holders, holders_v, small_sem.at[0]),
        pltpu.make_async_copy(traces.at[0], traces_v, small_sem.at[1]),
        pltpu.make_async_copy(aperture, aperture_v, small_sem.at[2]),
    ]
    owns = [
        pltpu.make_async_copy(adjoint.at[0, 0], back.at[0, pl.ds(4, 8)], own_sem.at[0]),
        pltpu.make_async_copy(adjoint.at[0, 1], back_old, own_sem.at[1]),
    ]
    own_model = [
        pltpu.make_async_copy(density, dens.at[s, pl.ds(8, 8)], local_sem.at[0]),
        pltpu.make_async_copy(velocity, speed.at[s, pl.ds(4, 8)], local_sem.at[1]),
        pltpu.make_async_copy(stored.at[b], pieces.at[b], local_sem.at[2]),
    ]

    barrier = pltpu.get_barrier_semaphore()

    def greet(step, carry):
        pl.semaphore_signal(barrier, inc=1, device_id={"gx": lax.rem(b + step, n_x)})
        return carry

    lax.fori_loop(1, n_x, greet, 0)

    def toward(dx, dy, shot=None):
        target = {} if shot is None else {"shot": shot}
        if dx:
            target["gx"] = lax.rem(b + n_x + dx, n_x)
        if dy:
            target["gy"] = lax.rem(j + n_y + dy, n_y)
        return target

    sides = ((1, 0), (-1, 0), (0, 1), (0, -1))
    diagonals = ((1, 1), (1, -1), (-1, 1), (-1, -1))
    near = [{"shot": other}]
    near += [toward(0, dy) for dy in (1, -1)]
    near += [toward(dx, dy) for dx, dy in diagonals]
    near += [toward(dx, dy, other) for dx, dy in sides + diagonals]
    for target in near:
        pl.semaphore_signal(barrier, inc=1, device_id=target)

    for copy in own_model + owns + smalls:
        copy.start()

    def fill(refs, value):
        for ref in refs:
            ref[...] = jnp.full(ref.shape, value, f32)

    @pl.when(b == 0)
    def _():
        fill((wide.at[:, :8], corner.at[:, :4], old.at[:4], back.at[:, :4], speed.at[:, :4]), 0.0)
        fill((dens.at[:, :8], dens_corner.at[:, :4]), 1.0)

    @pl.when(b == n_x - 1)
    def _():
        fill((wide.at[:, 16:], corner.at[:, 4:], old.at[12:], back.at[:, 12:], speed.at[:, 12:]), 0.0)
        fill((dens.at[:, 16:], dens_corner.at[:, 4:]), 1.0)

    @pl.when(j == 0)
    def _():
        fill((below, corner.at[:, :, 4:], old_y.at[:, 4:], back_y.at[:, :, 4:], speed_y.at[:, :, 4:]), 0.0)
        fill((dens_below, dens_corner.at[:, :, 4:]), 1.0)

    @pl.when(j == n_y - 1)
    def _():
        fill((above, corner.at[:, :, :4], old_y.at[:, :4], back_y.at[:, :, :4], speed_y.at[:, :, :4]), 0.0)
        fill((dens_above, dens_corner.at[:, :, :4]), 1.0)

    pl.semaphore_wait(barrier, n_x - 1 + len(near))

    def send_piece(step, carry):
        target = lax.rem(b + step, n_x)
        pltpu.make_async_remote_copy(
            stored.at[target], pieces.at[b], piece_send, piece_sem, device_id={"gx": target}
        ).start()
        return carry

    lax.fori_loop(1, n_x, send_piece, 0)

    def exists(dx, dy):
        there = b >= 0
        if dx:
            there &= (b < n_x - 1) if dx > 0 else (b > 0)
        if dy:
            there &= (j < n_y - 1) if dy > 0 else (j > 0)
        return there

    class Group:
        def __init__(self, entries, send_sem, recv_sem):
            self.items = []
            for at, (dx, dy, shot, src, dst) in enumerate(entries):
                copy = pltpu.make_async_remote_copy(
                    src, dst, send_sem.at[at], recv_sem.at[at], device_id=toward(dx, dy, shot)
                )
                self.items.append((copy, dx, dy))
            for copy, dx, dy in self.items:
                self.guard(dx, dy, copy.start)

        def guard(self, dx, dy, action):
            if dx or dy:
                pl.when(exists(dx, dy))(action)
            else:
                action()

        def received(self):
            for copy, dx, dy in self.items:
                self.guard(-dx, -dy, copy.wait_recv)

        def sent(self):
            for copy, dx, dy in self.items:
                self.guard(dx, dy, copy.wait_send)

    first, final = pl.ds(0, 4), pl.ds(4, 4)

    def shallow(src, base, planes, rows, shot=None):
        return [
            (1, 0, shot, src.at[pl.ds(base + 4, 4)], planes.at[pl.ds(0, 4)]),
            (-1, 0, shot, src.at[pl.ds(base, 4)], planes.at[pl.ds(12, 4)]),
            (0, 1, shot, src.at[pl.ds(base, 8), final], rows.at[:, final]),
            (0, -1, shot, src.at[pl.ds(base, 8), first], rows.at[:, first]),
        ]

    def deep(src, base, planes, lower, upper, corners, shot=None):
        whole = src.at[pl.ds(base, 8)]
        entries = [
            (1, 0, shot, whole, planes.at[pl.ds(0, 8)]),
            (-1, 0, shot, whole, planes.at[pl.ds(16, 8)]),
            (0, 1, shot, whole, lower),
            (0, -1, shot, whole, upper),
        ]
        for dx, dy in diagonals:
            rows = final if dy > 0 else first
            here = pl.ds(base + 4, 4) if dx > 0 else pl.ds(base, 4)
            there = first if dx > 0 else final
            entries.append((dx, dy, shot, src.at[here, rows], corners.at[there, rows]))
        return entries

    model = [
        (0, 0, other, density, dens.at[s, pl.ds(8, 8)]),
        (0, 0, other, velocity, speed.at[s, pl.ds(4, 8)]),
    ]
    for shot in (s, other):
        model += deep(
            density, 0, dens.at[s], dens_below.at[s], dens_above.at[s], dens_corner.at[s], shot
        )
        model += shallow(velocity, 0, speed.at[s], speed_y.at[s], shot)
    model = Group(model, model_send, model_recv)
    groups = [model]
    backs = [
        Group(
            shallow(adjoint.at[0, 0], 0, back.at[0], back_y.at[0]), back_send.at[0], back_recv.at[0]
        )
    ]

    row = lax.broadcasted_iota(jnp.int32, (1, 8, 128), 1)
    lane = lax.broadcasted_iota(jnp.int32, (1, 8, 128), 2)
    halves = (pl.ds(0, 128), pl.ds(128, 128))

    for copy in smalls:
        copy.wait()
    column = lax.broadcasted_iota(jnp.int32, (64, n_x), 0)
    place = column // 2
    parity = column - 2 * place
    hit = holders_v[...] == place
    picks = [jnp.where(hit & (parity == r), 1.0, 0.0).astype(f32) for r in range(2)]

    bounds = aperture_v[...]
    bounds = jnp.where(s == 0, bounds[0:1], bounds[1:2])
    active = jnp.where((b >= bounds[:, 0:1]) & (b < bounds[:, 1:2]), 1.0, 0.0).astype(f32)
    active = active.reshape(1, 1, 1)

    for copy in own_model[:2]:
        copy.wait()
    model.received()

    for half in range(2):
        dens[half] = jnp.log(dens[half])
        dens_below[half] = jnp.log(dens_below[half])
        dens_above[half] = jnp.log(dens_above[half])
        dens_corner[half] = jnp.log(dens_corner[half])

    def coefficients(out, count, speeds, logs, x_of, plus_of, minus_of):
        grads = [[0.0, 0.0, 0.0] for half in range(2)]
        for k in range(1, 5):
            tap = SLOPE_TAPS[k - 1]
            ahead = z_plus(logs[0], logs[1], lane, k)
            behind = z_minus(logs[0], logs[1], lane, k)
            ahead = (ahead[0], jnp.where(lane < 128 - k, ahead[1], 0.0))
            behind = (jnp.where(lane >= k, behind[0], 0.0), behind[1])
            for half in range(2):
                grads[half][0] += tap * (x_of(half, k) - x_of(half, -k))
                grads[half][1] += tap * (plus_of(half, k) - minus_of(half, k))
                grads[half][2] += tap * (ahead[half] - behind[half])
        for half, lanes in enumerate(halves):
            sq = speeds(half)
            sq = sq * sq
            out[0, :, :, lanes] = 2.0 + (3.0 * LAPLACE_TAPS[0]) * sq
            slopes = [sq * grad for grad in grads[half]]
            for k in range(1, 5):
                even = LAPLACE_TAPS[k] * sq
                for axis in range(3):
                    odd = SLOPE_TAPS[k - 1] * slopes[axis]
                    plus, minus = even - odd, even + odd
                    if axis == 2 and half == 0:
                        minus = jnp.where(lane >= k, minus, 0.0)
                    elif axis == 2:
                        plus = jnp.where(lane < 128 - k, plus, 0.0)
                    at = 1 + 6 * (k - 1) + 2 * axis
                    out[at, :, :, lanes] = plus
                    out[at + 1, :, :, lanes] = minus

    def ring_of(half):
        inner = jnp.where(row < 4, dens_above[half], dens_below[half])
        return jnp.concatenate([dens_corner[half, :4], inner, dens_corner[half, 4:]], axis=0)

    rings = [ring_of(half) for half in range(2)]
    coefficients(
        coef,
        16,
        lambda half: speed[half],
        [dens[half, 4:20] for half in range(2)],
        lambda half, k: dens[half, 4 + k : 20 + k],
        lambda half, k: y_plus(dens[half, 4:20], rings[half], row, k),
        lambda half, k: y_minus(dens[half, 4:20], rings[half], row, k),
    )

    eye = lax.broadcasted_iota(jnp.int32, (8, 8), 0) == lax.broadcasted_iota(jnp.int32, (8, 8), 1)
    at_receiver = lax.broadcasted_iota(jnp.int32, (8, 128), 1) == REC_Z
    for x in range(8):
        sq = speed[0, 4 + x] * speed[0, 4 + x]
        for number in range(STEPS):
            line = jnp.where(eye, traces_v[number, pl.ds(x, 1), :], 0.0)
            line = jnp.sum(line, axis=1, keepdims=True)
            inject[number, x] = jnp.where(at_receiver, line, 0.0) * sq

    def taps(table, planes, centre, x_of, plus_of, minus_of, before):
        total = [
            table[0, planes, :, lanes] * centre[half] - before[half]
            for half, lanes in enumerate(halves)
        ]
        for k in range(1, 5):
            at = 1 + 6 * (k - 1)
            ahead = z_plus(centre[0], centre[1], lane, k)
            behind = z_minus(centre[0], centre[1], lane, k)
            for half, lanes in enumerate(halves):
                total[half] = (
                    total[half]
                    + table[at, planes, :, lanes] * x_of(half, k)
                    + table[at + 1, planes, :, lanes] * x_of(half, -k)
                    + table[at + 2, planes, :, lanes] * plus_of(half, k)
                    + table[at + 3, planes, :, lanes] * minus_of(half, k)
                    + table[at + 4, planes, :, lanes] * ahead[half]
                    + table[at + 5, planes, :, lanes] * behind[half]
                )
        return total

    def block(ref, low, count):
        return [ref[low : low + count, :, lanes] for lanes in halves]

    def inner_step(planes, rows, before):
        centre, edge = block(planes, 4, 8), block(rows, 0, 8)
        return taps(
            coef,
            slice(4, 12),
            centre,
            lambda half, k: planes[4 + k : 12 + k, :, halves[half]],
            lambda half, k: y_plus(centre[half], edge[half], row, k),
            lambda half, k: y_minus(centre[half], edge[half], row, k),
            before,
        )

    def back_step(level):
        backs[level].received()
        before = block(back_old, 0, 8) if level == 0 else block(back.at[level - 1], 4, 8)
        new = inner_step(back.at[level], back_y.at[level], before)
        new[0] = new[0] + inject[STEPS - 1 - level]
        if level == STEPS - 1:
            for half, lanes in enumerate(halves):
                last[1, :, :, lanes] = new[half]
            return
        for half, lanes in enumerate(halves):
            back[level + 1, 4:12, :, lanes] = new[half]
        backs.append(
            Group(
                shallow(back.at[level + 1], 4, back.at[level + 1], back_y.at[level + 1]),
                back_send.at[level + 1],
                back_recv.at[level + 1],
            )
        )

    for copy in owns:
        copy.wait()
    back_step(0)

    coefficients(
        coef_y,
        8,
        lambda half: speed_y[half],
        [rings[half][4:12] for half in range(2)],
        lambda half, k: rings[half][4 + k : 12 + k],
        lambda half, k: y_plus_outer(
            dens[half, 8:16], dens_above[half], dens_below[half], row, k
        ),
        lambda half, k: y_minus_outer(
            dens[half, 8:16], dens_above[half], dens_below[half], row, k
        ),
    )

    def send_deep(level):
        group = Group(
            deep(
                wide.at[level],
                8,
                wide.at[level],
                below.at[level],
                above.at[level],
                corner.at[level],
            ),
            deep_send.at[level],
            deep_recv.at[level],
        )
        groups.append(group)
        return group

    own_model[2].wait()
    arrived = pieces.at[pl.ds(0, n_x - 1)]
    pltpu.make_async_copy(arrived, arrived, piece_sem).wait()
    for level in (0, 1):
        found = 0.0
        for r in range(2):
            found += jnp.dot(
                picks[r],
                pieces[:, level, r, :],
                precision=lax.Precision.HIGHEST,
                preferred_element_type=f32,
            )
        found = found.reshape(8, 8, 256)
        if level == 0:
            wide[0, 8:16] = found
            exchange = send_deep(0)
        else:
            old[4:12] = found
            old_group = Group(shallow(old, 4, old, old_y), old_send, old_recv)
            groups.append(old_group)

    def outer_step(level, before, before_y):
        planes, low, up = wide.at[level], below.at[level], above.at[level]
        for lanes in halves:
            ring[0:4, :, lanes] = corner[level, 0:4, :, lanes]
            ring[4:12, :, lanes] = jnp.where(row < 4, up[:, :, lanes], low[:, :, lanes])
            ring[12:16, :, lanes] = corner[level, 4:8, :, lanes]
        edge = block(ring, 4, 8)
        new = taps(
            coef_y,
            slice(0, 8),
            edge,
            lambda half, k: ring[4 + k : 12 + k, :, halves[half]],
            lambda half, k: y_plus_outer(
                planes[8:16, :, halves[half]], up[:, :, halves[half]], low[:, :, halves[half]], row, k
            ),
            lambda half, k: y_minus_outer(
                planes[8:16, :, halves[half]], up[:, :, halves[half]], low[:, :, halves[half]], row, k
            ),
            block(before_y, 0, 8),
        )
        for half, lanes in enumerate(halves):
            mid_y[level, :, :, lanes] = new[half]
        for start in (0, 8):
            centre, around = block(planes, 4 + start, 8), block(ring, start, 8)
            new = taps(
                coef,
                slice(start, start + 8),
                centre,
                lambda half, k: planes[4 + start + k : 12 + start + k, :, halves[half]],
                lambda half, k: y_plus(centre[half], around[half], row, k),
                lambda half, k: y_minus(centre[half], around[half], row, k),
                block(before, start, 8),
            )
            for half, lanes in enumerate(halves):
                mid[level, start : start + 8, :, lanes] = new[half]

    back_step(1)
    exchange.received()
    old_group.received()
    outer_step(0, old, old_y)
    new = inner_step(mid.at[0], mid_y.at[0], block(wide.at[0], 8, 8))
    for half, lanes in enumerate(halves):
        wide[1, 8:16, :, lanes] = new[half]
    exchange = send_deep(1)

    back_step(2)
    outs = [pltpu.make_async_copy(back.at[3, pl.ds(4, 8)], adjoint_out.at[0, 1], out_sem.at[0])]
    outs[0].start()
    early = [
        mid[0, 4:12, :, lanes] * back[3, 4:12, :, lanes]
        + wide[1, 8:16, :, lanes] * back[2, 4:12, :, lanes]
        for lanes in halves
    ]

    exchange.received()
    outer_step(1, mid.at[0], mid_y.at[0])
    outs.append(
        pltpu.make_async_copy(mid.at[1, pl.ds(4, 8)], forward_out.at[0, 1], out_sem.at[1])
    )
    outs[1].start()
    new = inner_step(mid.at[1], mid_y.at[1], block(wide.at[1], 8, 8))
    whole = [
        active
        * (
            early[half]
            + mid[1, 4:12, :, lanes] * back[1, 4:12, :, lanes]
            + new[half] * back[0, 4:12, :, lanes]
        )
        for half, lanes in enumerate(halves)
    ]
    share[...] = jnp.where(s == 0, whole[1], whole[0])
    to_partner = pltpu.make_async_remote_copy(
        share, partner_share, image_sem.at[0], image_sem.at[1], device_id={"shot": other}
    )
    to_partner.start()
    for half, lanes in enumerate(halves):
        last[0, :, :, lanes] = new[half]
    outs.append(pltpu.make_async_copy(last.at[0], forward_out.at[0, 0], out_sem.at[2]))
    outs[2].start()
    image_out[...] = jnp.where(s == 0, whole[0], whole[1])

    back_step(3)
    outs.append(pltpu.make_async_copy(last.at[1], adjoint_out.at[0, 0], out_sem.at[3]))
    outs[3].start()

    gone = stored.at[pl.ds(0, n_x - 1)]
    pltpu.make_async_copy(gone, gone, piece_send).wait()
    for group in groups + backs:
        group.sent()

    to_partner.wait()
    image_out[...] += partner_share[...]
    for copy in outs:
        copy.wait()


def finish(image, forward, adjoint, image_out, forward_out, adjoint_out, sem):
    copies = [
        pltpu.make_async_copy(src, dst, sem.at[at])
        for at, (src, dst) in enumerate(
            ((image, image_out), (forward, forward_out), (adjoint, adjoint_out))
        )
    ]
    for copy in copies:
        copy.start()
    for copy in copies:
        copy.wait()


def shards(n_x, n_y, velocity, density, stored, holders, adjoint, traces, aperture):
    f32 = jnp.float32
    anywhere = pl.BlockSpec(memory_space=pl.ANY)
    inside = pl.BlockSpec(memory_space=pltpu.VMEM)
    results = pl.pallas_call(
        functools.partial(kernel, n_x, n_y),
        out_shape=(
            pltpu.VMEM((8, 8, 128), f32),
            pltpu.VMEM((1, 2, 8, 8, 256), f32),
            pltpu.VMEM((1, 2, 8, 8, 256), f32),
        ),
        in_specs=[anywhere] * 7,
        out_specs=(inside,) * 3,
        scratch_shapes=[
            pltpu.VMEM((2, 24, 8, 256), f32),
            pltpu.VMEM((2, 8, 8, 256), f32),
            pltpu.VMEM((2, 8, 8, 256), f32),
            pltpu.VMEM((2, 8, 8, 256), f32),
            pltpu.VMEM((16, 8, 256), f32),
            pltpu.VMEM((2, 16, 8, 256), f32),
            pltpu.VMEM((2, 8, 8, 256), f32),
            pltpu.VMEM((16, 8, 256), f32),
            pltpu.VMEM((8, 8, 256), f32),
            pltpu.VMEM((STEPS, 16, 8, 256), f32),
            pltpu.VMEM((STEPS, 8, 8, 256), f32),
            pltpu.VMEM((8, 8, 256), f32),
            pltpu.VMEM((2, 8, 8, 256), f32),
            pltpu.VMEM((25, 16, 8, 256), f32),
            pltpu.VMEM((25, 8, 8, 256), f32),
            pltpu.VMEM((2, 24, 8, 128), f32),
            pltpu.VMEM((2, 8, 8, 128), f32),
            pltpu.VMEM((2, 8, 8, 128), f32),
            pltpu.VMEM((2, 8, 8, 128), f32),
            pltpu.VMEM((2, 16, 8, 128), f32),
            pltpu.VMEM((2, 8, 8, 128), f32),
            pltpu.VMEM((n_x, 2, 2, 256), f32),
            pltpu.VMEM((1, n_x), jnp.int32),
            pltpu.VMEM((STEPS, 8, 8), f32),
            pltpu.VMEM((2, 2), jnp.int32),
            pltpu.VMEM((STEPS, 8, 8, 128), f32),
            pltpu.VMEM((8, 8, 128), f32),
            pltpu.VMEM((8, 8, 128), f32),
            pltpu.SemaphoreType.DMA((3,)),
            pltpu.SemaphoreType.DMA((3,)),
            pltpu.SemaphoreType.DMA((2,)),
            pltpu.SemaphoreType.DMA,
            pltpu.SemaphoreType.DMA,
            pltpu.SemaphoreType.DMA((26,)),
            pltpu.SemaphoreType.DMA((26,)),
            pltpu.SemaphoreType.DMA((2, 8)),
            pltpu.SemaphoreType.DMA((2, 8)),
            pltpu.SemaphoreType.DMA((4,)),
            pltpu.SemaphoreType.DMA((4,)),
            pltpu.SemaphoreType.DMA((STEPS, 4)),
            pltpu.SemaphoreType.DMA((STEPS, 4)),
            pltpu.SemaphoreType.DMA((2,)),
            pltpu.SemaphoreType.DMA((4,)),
        ],
        compiler_params=pltpu.CompilerParams(
            collective_id=0, has_side_effects=True, vmem_limit_bytes=48 * 1024 * 1024
        ),
        cost_estimate=pl.CostEstimate(flops=8_000_000, bytes_accessed=800_000, transcendentals=0),
    )(*(
        pltpu.with_memory_space_constraint(given, pltpu.HBM)
        for given in (velocity, density, stored, holders, adjoint, traces, aperture)
    ))
    return pl.pallas_call(
        finish,
        out_shape=tuple(jax.ShapeDtypeStruct(one.shape, f32) for one in results),
        in_specs=[inside] * 3,
        out_specs=(anywhere,) * 3,
        scratch_shapes=[pltpu.SemaphoreType.DMA((3,))],
    )(*(pltpu.with_memory_space_constraint(one, pltpu.VMEM) for one in results))


def solution(mesh):
    return jax.shard_map(
        functools.partial(shards, mesh.shape["gx"], mesh.shape["gy"]),
        mesh=mesh,
        in_specs=(
            P("gx", "gy", "shot"),
            P("gx", "gy", "shot"),
            P("gx", None, ("shot", "gy"), None),
            P("gx", None),
            P("shot", None, "gx", "gy", None),
            P("shot", None, "gx", "gy"),
            P(),
        ),
        out_specs=(
            P("gx", "gy", "shot"),
            P("shot", None, "gx", "gy", None),
            P("shot", None, "gx", "gy", None),
        ),
        check_vma=False,
    )
```

time: 43.1 us -> 46.1 us (1.070)
  the two profiles are of different devices: /device:TPU:18 before, /device:TPU:2 now
where the time goes in v3:
time: 46.1 us; the launch traced here: 46 us
  Pallas kernels  45.4 us (98%)
  between operations  0.64 us (1%)
    pallas_call x1, Pallas kernels, shards(): pl.pallas_call(functools.partial(kernel, n_x, n_y), out_shape=(pltpu.VMEM...  44.6 us

profile of v3, /device:TPU:2, one launch (start us, length us, event | category | flops | bytes accessed | tf_op | source)
XLA Modules:
  0.0 46.0 jit_solution(5211546321310733481)
XLA Ops:
  0.6 44.6 %shard_map.94 = (f32[8,8,128]{2,1,0:T(8,128)S(1)}, f32[1,2,8,8,256]{4,3,2,1,0:T(8,128)S(1)}, f32[1,2,8,8,256]{4,3,2,1,0:T(8,128)S(1)}) custom-call(f32[8,8,128]{2,1,0:T(8,128)} %velocity.1, f32[8,8,128]{2,1,0:T(8,128)} %density.1, f32[32,2,2,256]{3,2,1,0:T(2,128)} %stored.1, s32[1,32]{1,0:T(1,128)} %holders.1, f32[1,2,8,8,256]{4,3,2,1,0:T(8,128)} %adjoint.1, ...), custom_call_target="tpu_custom_call" | custom-call | flops 8000000 | bytes 800000 | tf_op jit(solution)/shard_map/pallas_call | solution.py:562
  45.3 0.7 %shard_map.95 = (f32[8,8,128]{2,1,0:T(8,128)}, f32[1,2,8,8,256]{4,3,2,1,0:T(8,128)}, f32[1,2,8,8,256]{4,3,2,1,0:T(8,128)}) custom-call(f32[8,8,128]{2,1,0:T(8,128)S(1)} %get-tuple-element.6.image, f32[1,2,8,8,256]{4,3,2,1,0:T(8,128)S(1)} %get-tuple-element.7.forward, f32[1,2,8,8,256]{4,3,2,1,0:T(8,128)S(1)} %get-tuple-element.8.adjoint), custom_call_target="tpu_custom_call" | custom-call | tf_op jit(solution)/shard_map/pallas_call | solution.py:624

commit v4 on v3

--- a/solution.py
+++ b/solution.py
@@ -54,6 +54,8 @@
     image_out,
     forward_out,
     adjoint_out,
+    ahead,
+    ahead_y,
     wide,
     below,
     above,
@@ -62,7 +64,6 @@
     mid,
     mid_y,
     old,
-    old_y,
     back,
     back_y,
     back_old,
@@ -70,9 +71,8 @@
     coef,
     coef_y,
     dens,
-    dens_below,
-    dens_above,
-    dens_corner,
+    dens_ring,
+    dens_far,
     speed,
     speed_y,
     pieces,
@@ -89,10 +89,12 @@
     piece_send,
     model_send,
     model_recv,
+    outer_send,
+    outer_recv,
     deep_send,
     deep_recv,
-    old_send,
-    old_recv,
+    ahead_send,
+    ahead_recv,
     back_send,
     back_recv,
     image_sem,
@@ -151,23 +153,23 @@
 
     @pl.when(b == 0)
     def _():
-        fill((wide.at[:, :8], corner.at[:, :4], old.at[:4], back.at[:, :4], speed.at[:, :4]), 0.0)
-        fill((dens.at[:, :8], dens_corner.at[:, :4]), 1.0)
+        fill((wide.at[:8], corner.at[:4], ahead.at[:, :4], back.at[:, :4], speed.at[:, :4]), 0.0)
+        fill((dens.at[:, :8], dens_ring.at[:, :4]), 1.0)
 
     @pl.when(b == n_x - 1)
     def _():
-        fill((wide.at[:, 16:], corner.at[:, 4:], old.at[12:], back.at[:, 12:], speed.at[:, 12:]), 0.0)
-        fill((dens.at[:, 16:], dens_corner.at[:, 4:]), 1.0)
+        fill((wide.at[16:], corner.at[4:], ahead.at[:, 12:], back.at[:, 12:], speed.at[:, 12:]), 0.0)
+        fill((dens.at[:, 16:], dens_ring.at[:, 12:]), 1.0)
 
     @pl.when(j == 0)
     def _():
-        fill((below, corner.at[:, :, 4:], old_y.at[:, 4:], back_y.at[:, :, 4:], speed_y.at[:, :, 4:]), 0.0)
-        fill((dens_below, dens_corner.at[:, :, 4:]), 1.0)
+        fill((below, corner.at[:, 4:], ahead_y.at[:, :, 4:], back_y.at[:, :, 4:], speed_y.at[:, :, 4:]), 0.0)
+        fill((dens_far.at[:, :, :4], dens_ring.at[:, :, 4:]), 1.0)
 
     @pl.when(j == n_y - 1)
     def _():
-        fill((above, corner.at[:, :, :4], old_y.at[:, :4], back_y.at[:, :, :4], speed_y.at[:, :, :4]), 0.0)
-        fill((dens_above, dens_corner.at[:, :, :4]), 1.0)
+        fill((above, corner.at[:, :4], ahead_y.at[:, :, :4], back_y.at[:, :, :4], speed_y.at[:, :, :4]), 0.0)
+        fill((dens_far.at[:, :, 4:], dens_ring.at[:, :, :4]), 1.0)
 
     pl.semaphore_wait(barrier, n_x - 1 + len(near))
 
@@ -228,32 +230,43 @@
         entries = [
             (1, 0, shot, whole, planes.at[pl.ds(0, 8)]),
             (-1, 0, shot, whole, planes.at[pl.ds(16, 8)]),
-            (0, 1, shot, whole, lower),
-            (0, -1, shot, whole, upper),
         ]
         for dx, dy in diagonals:
             rows = final if dy > 0 else first
             here = pl.ds(base + 4, 4) if dx > 0 else pl.ds(base, 4)
             there = first if dx > 0 else final
             entries.append((dx, dy, shot, src.at[here, rows], corners.at[there, rows]))
+        entries.append((0, 1, shot, whole, lower))
+        entries.append((0, -1, shot, whole, upper))
         return entries
 
-    model = [
-        (0, 0, other, density, dens.at[s, pl.ds(8, 8)]),
-        (0, 0, other, velocity, speed.at[s, pl.ds(4, 8)]),
-    ]
-    for shot in (s, other):
-        model += deep(
-            density, 0, dens.at[s], dens_below.at[s], dens_above.at[s], dens_corner.at[s], shot
-        )
-        model += shallow(velocity, 0, speed.at[s], speed_y.at[s], shot)
-    model = Group(model, model_send, model_recv)
-    groups = [model]
     backs = [
         Group(
             shallow(adjoint.at[0, 0], 0, back.at[0], back_y.at[0]), back_send.at[0], back_recv.at[0]
         )
     ]
+
+    model = [
+        (0, 0, other, density, dens.at[s, pl.ds(8, 8)]),
+        (0, 0, other, velocity, speed.at[s, pl.ds(4, 8)]),
+    ]
+    outer_model = []
+    for shot in (s, other):
+        ring_s = dens_ring.at[s]
+        model += shallow(density, 0, dens.at[s, pl.ds(4, 16)], ring_s.at[pl.ds(4, 8)], shot)
+        outer_model += shallow(velocity, 0, speed.at[s], speed_y.at[s], shot)
+        outer_model += [
+            (1, 0, shot, density.at[first], dens.at[s, pl.ds(0, 4)]),
+            (-1, 0, shot, density.at[final], dens.at[s, pl.ds(20, 4)]),
+            (0, 1, shot, density.at[:, first], dens_far.at[s, :, first]),
+            (0, -1, shot, density.at[:, final], dens_far.at[s, :, final]),
+        ]
+        for dx, dy in diagonals:
+            rows = final if dy > 0 else first
+            here, there = (final, first) if dx > 0 else (first, pl.ds(12, 4))
+            outer_model.append((dx, dy, shot, density.at[here, rows], ring_s.at[there, rows]))
+    model = Group(model, model_send, model_recv)
+    groups = [model]
 
     row = lax.broadcasted_iota(jnp.int32, (1, 8, 128), 1)
     lane = lax.broadcasted_iota(jnp.int32, (1, 8, 128), 2)
@@ -272,17 +285,13 @@
     active = jnp.where((b >= bounds[:, 0:1]) & (b < bounds[:, 1:2]), 1.0, 0.0).astype(f32)
     active = active.reshape(1, 1, 1)
 
-    for copy in own_model[:2]:
-        copy.wait()
-    model.received()
-
-    for half in range(2):
-        dens[half] = jnp.log(dens[half])
-        dens_below[half] = jnp.log(dens_below[half])
-        dens_above[half] = jnp.log(dens_above[half])
-        dens_corner[half] = jnp.log(dens_corner[half])
-
-    def coefficients(out, count, speeds, logs, x_of, plus_of, minus_of):
+    def coefficients(out, parts, speeds, logs, x_of, plus_of, minus_of):
+        def put(at, lanes, value):
+            start = 0
+            for low, count in parts:
+                out[at, low : low + count, :, lanes] = value[start : start + count]
+                start += count
+
         grads = [[0.0, 0.0, 0.0] for half in range(2)]
         for k in range(1, 5):
             tap = SLOPE_TAPS[k - 1]
@@ -297,7 +306,7 @@
         for half, lanes in enumerate(halves):
             sq = speeds(half)
             sq = sq * sq
-            out[0, :, :, lanes] = 2.0 + (3.0 * LAPLACE_TAPS[0]) * sq
+            put(0, lanes, 2.0 + (3.0 * LAPLACE_TAPS[0]) * sq)
             slopes = [sq * grad for grad in grads[half]]
             for k in range(1, 5):
                 even = LAPLACE_TAPS[k] * sq
@@ -309,118 +318,86 @@
                     elif axis == 2:
                         plus = jnp.where(lane < 128 - k, plus, 0.0)
                     at = 1 + 6 * (k - 1) + 2 * axis
-                    out[at, :, :, lanes] = plus
-                    out[at + 1, :, :, lanes] = minus
-
-    def ring_of(half):
-        inner = jnp.where(row < 4, dens_above[half], dens_below[half])
-        return jnp.concatenate([dens_corner[half, :4], inner, dens_corner[half, 4:]], axis=0)
-
-    rings = [ring_of(half) for half in range(2)]
-    coefficients(
-        coef,
-        16,
-        lambda half: speed[half],
-        [dens[half, 4:20] for half in range(2)],
-        lambda half, k: dens[half, 4 + k : 20 + k],
-        lambda half, k: y_plus(dens[half, 4:20], rings[half], row, k),
-        lambda half, k: y_minus(dens[half, 4:20], rings[half], row, k),
-    )
-
-    eye = lax.broadcasted_iota(jnp.int32, (8, 8), 0) == lax.broadcasted_iota(jnp.int32, (8, 8), 1)
-    at_receiver = lax.broadcasted_iota(jnp.int32, (8, 128), 1) == REC_Z
-    for x in range(8):
-        sq = speed[0, 4 + x] * speed[0, 4 + x]
-        for number in range(STEPS):
-            line = jnp.where(eye, traces_v[number, pl.ds(x, 1), :], 0.0)
-            line = jnp.sum(line, axis=1, keepdims=True)
-            inject[number, x] = jnp.where(at_receiver, line, 0.0) * sq
-
-    def taps(table, planes, centre, x_of, plus_of, minus_of, before):
-        total = [
-            table[0, planes, :, lanes] * centre[half] - before[half]
-            for half, lanes in enumerate(halves)
-        ]
-        for k in range(1, 5):
-            at = 1 + 6 * (k - 1)
-            ahead = z_plus(centre[0], centre[1], lane, k)
-            behind = z_minus(centre[0], centre[1], lane, k)
+                    put(at, lanes, plus)
+                    put(at + 1, lanes, minus)
+
+    def steps(count, table, base, centre_of, x_of, plus_of, minus_of, before_of, put):
+        def one(p, carry):
+            centre = [centre_of(p, lanes) for lanes in halves]
+            place = pl.ds(base + p, 1)
+            total = [
+                table[0, place, :, lanes] * centre[half] - before_of(p, lanes)
+                for half, lanes in enumerate(halves)
+            ]
+            for k in range(1, 5):
+                at = 1 + 6 * (k - 1)
+                up = z_plus(centre[0], centre[1], lane, k)
+                down = z_minus(centre[0], centre[1], lane, k)
+                for half, lanes in enumerate(halves):
+                    total[half] = (
+                        total[half]
+                        + table[at, place, :, lanes] * x_of(p, lanes, k)
+                        + table[at + 1, place, :, lanes] * x_of(p, lanes, -k)
+                        + table[at + 2, place, :, lanes] * plus_of(p, lanes, centre[half], k)
+                        + table[at + 3, place, :, lanes] * minus_of(p, lanes, centre[half], k)
+                        + table[at + 4, place, :, lanes] * up[half]
+                        + table[at + 5, place, :, lanes] * down[half]
+                    )
             for half, lanes in enumerate(halves):
-                total[half] = (
-                    total[half]
-                    + table[at, planes, :, lanes] * x_of(half, k)
-                    + table[at + 1, planes, :, lanes] * x_of(half, -k)
-                    + table[at + 2, planes, :, lanes] * plus_of(half, k)
-                    + table[at + 3, planes, :, lanes] * minus_of(half, k)
-                    + table[at + 4, planes, :, lanes] * ahead[half]
-                    + table[at + 5, planes, :, lanes] * behind[half]
-                )
-        return total
-
-    def block(ref, low, count):
-        return [ref[low : low + count, :, lanes] for lanes in halves]
-
-    def inner_step(planes, rows, before):
-        centre, edge = block(planes, 4, 8), block(rows, 0, 8)
-        return taps(
+                put(p, lanes, total[half], half)
+            return carry
+
+        lax.fori_loop(0, count, one, 0, unroll=True)
+
+    def into(ref, base):
+        def put(p, lanes, value, half):
+            ref[pl.ds(base + p, 1), :, lanes] = value
+
+        return put
+
+    def plane_of(ref, base):
+        return lambda p, lanes, k=0: ref[pl.ds(base + p + k, 1), :, lanes]
+
+    def inner_step(planes, rows, before, put, base=4, first_row=0):
+        edge = plane_of(rows, first_row)
+        steps(
+            8,
             coef,
-            slice(4, 12),
-            centre,
-            lambda half, k: planes[4 + k : 12 + k, :, halves[half]],
-            lambda half, k: y_plus(centre[half], edge[half], row, k),
-            lambda half, k: y_minus(centre[half], edge[half], row, k),
+            base,
+            plane_of(planes, base),
+            plane_of(planes, base),
+            lambda p, lanes, centre, k: y_plus(centre, edge(p, lanes), row, k),
+            lambda p, lanes, centre, k: y_minus(centre, edge(p, lanes), row, k),
             before,
+            put,
         )
 
     def back_step(level):
         backs[level].received()
-        before = block(back_old, 0, 8) if level == 0 else block(back.at[level - 1], 4, 8)
-        new = inner_step(back.at[level], back_y.at[level], before)
-        new[0] = new[0] + inject[STEPS - 1 - level]
-        if level == STEPS - 1:
-            for half, lanes in enumerate(halves):
-                last[1, :, :, lanes] = new[half]
-            return
-        for half, lanes in enumerate(halves):
-            back[level + 1, 4:12, :, lanes] = new[half]
-        backs.append(
-            Group(
-                shallow(back.at[level + 1], 4, back.at[level + 1], back_y.at[level + 1]),
-                back_send.at[level + 1],
-                back_recv.at[level + 1],
+        before = plane_of(back_old, 0) if level == 0 else plane_of(back.at[level - 1], 4)
+        target = last.at[1] if level == STEPS - 1 else back.at[level + 1]
+        start = 0 if level == STEPS - 1 else 4
+
+        def put(p, lanes, value, half):
+            if half == 0:
+                value = value + inject[STEPS - 1 - level, pl.ds(p, 1)]
+            target[pl.ds(start + p, 1), :, lanes] = value
+
+        inner_step(back.at[level], back_y.at[level], before, put)
+        if level < STEPS - 1:
+            backs.append(
+                Group(
+                    shallow(back.at[level + 1], 4, back.at[level + 1], back_y.at[level + 1]),
+                    back_send.at[level + 1],
+                    back_recv.at[level + 1],
+                )
             )
-        )
-
-    for copy in owns:
-        copy.wait()
-    back_step(0)
-
-    coefficients(
-        coef_y,
-        8,
-        lambda half: speed_y[half],
-        [rings[half][4:12] for half in range(2)],
-        lambda half, k: rings[half][4 + k : 12 + k],
-        lambda half, k: y_plus_outer(
-            dens[half, 8:16], dens_above[half], dens_below[half], row, k
-        ),
-        lambda half, k: y_minus_outer(
-            dens[half, 8:16], dens_above[half], dens_below[half], row, k
-        ),
-    )
-
-    def send_deep(level):
+
+    def send_ahead(level):
         group = Group(
-            deep(
-                wide.at[level],
-                8,
-                wide.at[level],
-                below.at[level],
-                above.at[level],
-                corner.at[level],
-            ),
-            deep_send.at[level],
-            deep_recv.at[level],
+            shallow(ahead.at[level], 4, ahead.at[level], ahead_y.at[level]),
+            ahead_send.at[level],
+            ahead_recv.at[level],
         )
         groups.append(group)
         return group
@@ -439,80 +416,138 @@
             )
         found = found.reshape(8, 8, 256)
         if level == 0:
-            wide[0, 8:16] = found
-            exchange = send_deep(0)
+            ahead[0, 4:12] = found
+            exchange = send_ahead(0)
         else:
-            old[4:12] = found
-            old_group = Group(shallow(old, 4, old, old_y), old_send, old_recv)
-            groups.append(old_group)
-
-    def outer_step(level, before, before_y):
-        planes, low, up = wide.at[level], below.at[level], above.at[level]
-        for lanes in halves:
-            ring[0:4, :, lanes] = corner[level, 0:4, :, lanes]
-            ring[4:12, :, lanes] = jnp.where(row < 4, up[:, :, lanes], low[:, :, lanes])
-            ring[12:16, :, lanes] = corner[level, 4:8, :, lanes]
-        edge = block(ring, 4, 8)
-        new = taps(
-            coef_y,
-            slice(0, 8),
-            edge,
-            lambda half, k: ring[4 + k : 12 + k, :, halves[half]],
-            lambda half, k: y_plus_outer(
-                planes[8:16, :, halves[half]], up[:, :, halves[half]], low[:, :, halves[half]], row, k
-            ),
-            lambda half, k: y_minus_outer(
-                planes[8:16, :, halves[half]], up[:, :, halves[half]], low[:, :, halves[half]], row, k
-            ),
-            block(before_y, 0, 8),
-        )
-        for half, lanes in enumerate(halves):
-            mid_y[level, :, :, lanes] = new[half]
-        for start in (0, 8):
-            centre, around = block(planes, 4 + start, 8), block(ring, start, 8)
-            new = taps(
-                coef,
-                slice(start, start + 8),
-                centre,
-                lambda half, k: planes[4 + start + k : 12 + start + k, :, halves[half]],
-                lambda half, k: y_plus(centre[half], around[half], row, k),
-                lambda half, k: y_minus(centre[half], around[half], row, k),
-                block(before, start, 8),
-            )
-            for half, lanes in enumerate(halves):
-                mid[level, start : start + 8, :, lanes] = new[half]
-
+            old[...] = found
+
+    for copy in own_model[:2]:
+        copy.wait()
+    model.received()
+    for half in range(2):
+        dens[half, 4:20] = jnp.log(dens[half, 4:20])
+        dens_ring[half, 4:12] = jnp.log(dens_ring[half, 4:12])
+    coefficients(
+        coef,
+        ((4, 8),),
+        lambda half: speed[half, 4:12],
+        [dens[half, 8:16] for half in range(2)],
+        lambda half, k: dens[half, 8 + k : 16 + k],
+        lambda half, k: y_plus(dens[half, 8:16], dens_ring[half, 4:12], row, k),
+        lambda half, k: y_minus(dens[half, 8:16], dens_ring[half, 4:12], row, k),
+    )
+    eye = lax.broadcasted_iota(jnp.int32, (8, 8), 0) == lax.broadcasted_iota(jnp.int32, (8, 8), 1)
+    at_receiver = lax.broadcasted_iota(jnp.int32, (8, 128), 1) == REC_Z
+    for x in range(8):
+        sq = speed[0, 4 + x] * speed[0, 4 + x]
+        for number in range(STEPS):
+            line = jnp.where(eye, traces_v[number, pl.ds(x, 1), :], 0.0)
+            line = jnp.sum(line, axis=1, keepdims=True)
+            inject[number, x] = jnp.where(at_receiver, line, 0.0) * sq
+
+    for copy in owns:
+        copy.wait()
+    back_step(0)
+
+    outer_model = Group(outer_model, outer_send, outer_recv)
+    groups.append(outer_model)
+
+    exchange.received()
+    inner_step(ahead.at[0], ahead_y.at[0], plane_of(old, 0), into(ahead.at[1], 4))
+    exchange = send_ahead(1)
     back_step(1)
     exchange.received()
-    old_group.received()
-    outer_step(0, old, old_y)
-    new = inner_step(mid.at[0], mid_y.at[0], block(wide.at[0], 8, 8))
-    for half, lanes in enumerate(halves):
-        wide[1, 8:16, :, lanes] = new[half]
-    exchange = send_deep(1)
+    inner_step(ahead.at[1], ahead_y.at[1], plane_of(ahead.at[0], 4), into(wide, 8))
+    exchange = Group(deep(wide, 8, wide, below, above, corner), deep_send, deep_recv)
+    groups.append(exchange)
+
+    outer_model.received()
+    for half in range(2):
+        for planes in (slice(0, 4), slice(20, 24)):
+            dens[half, planes] = jnp.log(dens[half, planes])
+        for planes in (slice(0, 4), slice(12, 16)):
+            dens_ring[half, planes] = jnp.log(dens_ring[half, planes])
+        dens_far[half] = jnp.log(dens_far[half])
+
+    def both(ref, half, low, high):
+        return jnp.concatenate([ref[half, low : low + 4], ref[half, high : high + 4]], axis=0)
+
+    coefficients(
+        coef,
+        ((0, 4), (12, 4)),
+        lambda half: both(speed, half, 0, 12),
+        [both(dens, half, 4, 16) for half in range(2)],
+        lambda half, k: both(dens, half, 4 + k, 16 + k),
+        lambda half, k: y_plus(both(dens, half, 4, 16), both(dens_ring, half, 0, 12), row, k),
+        lambda half, k: y_minus(both(dens, half, 4, 16), both(dens_ring, half, 0, 12), row, k),
+    )
+    dens_above = [
+        jnp.where(row < 4, dens_ring[half, 4:12], dens_far[half]) for half in range(2)
+    ]
+    dens_below = [
+        jnp.where(row < 4, dens_far[half], dens_ring[half, 4:12]) for half in range(2)
+    ]
+    coefficients(
+        coef_y,
+        ((0, 8),),
+        lambda half: speed_y[half],
+        [dens_ring[half, 4:12] for half in range(2)],
+        lambda half, k: dens_ring[half, 4 + k : 12 + k],
+        lambda half, k: y_plus_outer(dens[half, 8:16], dens_above[half], dens_below[half], row, k),
+        lambda half, k: y_minus_outer(dens[half, 8:16], dens_above[half], dens_below[half], row, k),
+    )
 
     back_step(2)
     outs = [pltpu.make_async_copy(back.at[3, pl.ds(4, 8)], adjoint_out.at[0, 1], out_sem.at[0])]
     outs[0].start()
     early = [
-        mid[0, 4:12, :, lanes] * back[3, 4:12, :, lanes]
-        + wide[1, 8:16, :, lanes] * back[2, 4:12, :, lanes]
+        ahead[1, 4:12, :, lanes] * back[3, 4:12, :, lanes]
+        + wide[8:16, :, lanes] * back[2, 4:12, :, lanes]
         for lanes in halves
     ]
 
     exchange.received()
-    outer_step(1, mid.at[0], mid_y.at[0])
-    outs.append(
-        pltpu.make_async_copy(mid.at[1, pl.ds(4, 8)], forward_out.at[0, 1], out_sem.at[1])
-    )
+    for lanes in halves:
+        ring[0:4, :, lanes] = corner[0:4, :, lanes]
+        ring[4:12, :, lanes] = jnp.where(row < 4, above[:, :, lanes], below[:, :, lanes])
+        ring[12:16, :, lanes] = corner[4:8, :, lanes]
+    low, mine, up = plane_of(below, 0), plane_of(wide, 8), plane_of(above, 0)
+    steps(
+        8,
+        coef_y,
+        0,
+        plane_of(ring, 4),
+        plane_of(ring, 4),
+        lambda p, lanes, centre, k: y_plus_outer(
+            mine(p, lanes), up(p, lanes), low(p, lanes), row, k
+        ),
+        lambda p, lanes, centre, k: y_minus_outer(
+            mine(p, lanes), up(p, lanes), low(p, lanes), row, k
+        ),
+        plane_of(ahead_y.at[1], 0),
+        into(mid_y, 0),
+    )
+    around = plane_of(ring, 0)
+    steps(
+        16,
+        coef,
+        0,
+        plane_of(wide, 4),
+        plane_of(wide, 4),
+        lambda p, lanes, centre, k: y_plus(centre, around(p, lanes), row, k),
+        lambda p, lanes, centre, k: y_minus(centre, around(p, lanes), row, k),
+        plane_of(ahead.at[1], 0),
+        into(mid, 0),
+    )
+    outs.append(pltpu.make_async_copy(mid.at[pl.ds(4, 8)], forward_out.at[0, 1], out_sem.at[1]))
     outs[1].start()
-    new = inner_step(mid.at[1], mid_y.at[1], block(wide.at[1], 8, 8))
+    inner_step(mid, mid_y, plane_of(wide, 8), into(last.at[0], 0))
     whole = [
         active
         * (
             early[half]
-            + mid[1, 4:12, :, lanes] * back[1, 4:12, :, lanes]
-            + new[half] * back[0, 4:12, :, lanes]
+            + mid[4:12, :, lanes] * back[1, 4:12, :, lanes]
+            + last[0, :, :, lanes] * back[0, 4:12, :, lanes]
         )
         for half, lanes in enumerate(halves)
     ]
@@ -521,8 +556,6 @@
         share, partner_share, image_sem.at[0], image_sem.at[1], device_id={"shot": other}
     )
     to_partner.start()
-    for half, lanes in enumerate(halves):
-        last[0, :, :, lanes] = new[half]
     outs.append(pltpu.make_async_copy(last.at[0], forward_out.at[0, 0], out_sem.at[2]))
     outs[2].start()
     image_out[...] = jnp.where(s == 0, whole[0], whole[1])
@@ -569,14 +602,15 @@
         in_specs=[anywhere] * 7,
         out_specs=(inside,) * 3,
         scratch_shapes=[
-            pltpu.VMEM((2, 24, 8, 256), f32),
-            pltpu.VMEM((2, 8, 8, 256), f32),
-            pltpu.VMEM((2, 8, 8, 256), f32),
-            pltpu.VMEM((2, 8, 8, 256), f32),
-            pltpu.VMEM((16, 8, 256), f32),
             pltpu.VMEM((2, 16, 8, 256), f32),
             pltpu.VMEM((2, 8, 8, 256), f32),
+            pltpu.VMEM((24, 8, 256), f32),
+            pltpu.VMEM((8, 8, 256), f32),
+            pltpu.VMEM((8, 8, 256), f32),
+            pltpu.VMEM((8, 8, 256), f32),
             pltpu.VMEM((16, 8, 256), f32),
+            pltpu.VMEM((16, 8, 256), f32),
+            pltpu.VMEM((8, 8, 256), f32),
             pltpu.VMEM((8, 8, 256), f32),
             pltpu.VMEM((STEPS, 16, 8, 256), f32),
             pltpu.VMEM((STEPS, 8, 8, 256), f32),
@@ -585,8 +619,7 @@
             pltpu.VMEM((25, 16, 8, 256), f32),
             pltpu.VMEM((25, 8, 8, 256), f32),
             pltpu.VMEM((2, 24, 8, 128), f32),
-            pltpu.VMEM((2, 8, 8, 128), f32),
-            pltpu.VMEM((2, 8, 8, 128), f32),
+            pltpu.VMEM((2, 16, 8, 128), f32),
             pltpu.VMEM((2, 8, 8, 128), f32),
             pltpu.VMEM((2, 16, 8, 128), f32),
             pltpu.VMEM((2, 8, 8, 128), f32),
@@ -602,12 +635,14 @@
             pltpu.SemaphoreType.DMA((2,)),
             pltpu.SemaphoreType.DMA,
             pltpu.SemaphoreType.DMA,
-            pltpu.SemaphoreType.DMA((26,)),
-            pltpu.SemaphoreType.DMA((26,)),
-            pltpu.SemaphoreType.DMA((2, 8)),
-            pltpu.SemaphoreType.DMA((2, 8)),
-            pltpu.SemaphoreType.DMA((4,)),
-            pltpu.SemaphoreType.DMA((4,)),
+            pltpu.SemaphoreType.DMA((10,)),
+            pltpu.SemaphoreType.DMA((10,)),
+            pltpu.SemaphoreType.DMA((24,)),
+            pltpu.SemaphoreType.DMA((24,)),
+            pltpu.SemaphoreType.DMA((8,)),
+            pltpu.SemaphoreType.DMA((8,)),
+            pltpu.SemaphoreType.DMA((2, 4)),
+            pltpu.SemaphoreType.DMA((2, 4)),
             pltpu.SemaphoreType.DMA((STEPS, 4)),
             pltpu.SemaphoreType.DMA((STEPS, 4)),
             pltpu.SemaphoreType.DMA((2,)),

time: 46.1 us -> 41.4 us (0.90)
  the two profiles are of different devices: /device:TPU:2 before, /device:TPU:10 now
where the time goes in v4:
time: 41.4 us; the launch traced here: 41.3 us
  Pallas kernels  40.7 us (98%)
  between operations  0.64 us (2%)
    pallas_call x1, Pallas kernels, shards(): pl.pallas_call(functools.partial(kernel, n_x, n_y), out_shape=(pltpu.VMEM...  39.9 us

profile of v4, /device:TPU:10, one launch (start us, length us, event | category | flops | bytes accessed | tf_op | source)
XLA Modules:
  0.0 41.3 jit_solution(7885991218524466778)
XLA Ops:
  0.6 39.9 %shard_map.94 = (f32[8,8,128]{2,1,0:T(8,128)S(1)}, f32[1,2,8,8,256]{4,3,2,1,0:T(8,128)S(1)}, f32[1,2,8,8,256]{4,3,2,1,0:T(8,128)S(1)}) custom-call(f32[8,8,128]{2,1,0:T(8,128)} %velocity.1, f32[8,8,128]{2,1,0:T(8,128)} %density.1, f32[32,2,2,256]{3,2,1,0:T(2,128)} %stored.1, s32[1,32]{1,0:T(1,128)} %holders.1, f32[1,2,8,8,256]{4,3,2,1,0:T(8,128)} %adjoint.1, ...), custom_call_target="tpu_custom_call" | custom-call | flops 8000000 | bytes 800000 | tf_op jit(solution)/shard_map/pallas_call | solution.py:595
  40.6 0.7 %shard_map.95 = (f32[8,8,128]{2,1,0:T(8,128)}, f32[1,2,8,8,256]{4,3,2,1,0:T(8,128)}, f32[1,2,8,8,256]{4,3,2,1,0:T(8,128)}) custom-call(f32[8,8,128]{2,1,0:T(8,128)S(1)} %get-tuple-element.6.image, f32[1,2,8,8,256]{4,3,2,1,0:T(8,128)S(1)} %get-tuple-element.7.forward, f32[1,2,8,8,256]{4,3,2,1,0:T(8,128)S(1)} %get-tuple-element.8.adjoint), custom_call_target="tpu_custom_call" | custom-call | tf_op jit(solution)/shard_map/pallas_call | solution.py:659

commit v5 on v4

--- a/solution.py
+++ b/solution.py
@@ -91,6 +91,8 @@
     model_recv,
     outer_send,
     outer_recv,
+    hand_send,
+    hand_recv,
     deep_send,
     deep_recv,
     ahead_send,
@@ -140,7 +142,7 @@
     near = [{"shot": other}]
     near += [toward(0, dy) for dy in (1, -1)]
     near += [toward(dx, dy) for dx, dy in diagonals]
-    near += [toward(dx, dy, other) for dx, dy in sides + diagonals]
+    near += [toward(dx, dy, other) for dx, dy in sides]
     for target in near:
         pl.semaphore_signal(barrier, inc=1, device_id=target)
 
@@ -151,25 +153,34 @@
         for ref in refs:
             ref[...] = jnp.full(ref.shape, value, f32)
 
+    low4, high4 = pl.ds(0, 4), pl.ds(4, 4)
+
     @pl.when(b == 0)
     def _():
-        fill((wide.at[:8], corner.at[:4], ahead.at[:, :4], back.at[:, :4], speed.at[:, :4]), 0.0)
-        fill((dens.at[:, :8], dens_ring.at[:, :4]), 1.0)
+        fill((wide.at[:8], corner.at[:4], ahead.at[:, :4], back.at[:, :4], speed.at[s, low4]), 0.0)
+        fill((dens.at[:, 4:8],), 1.0)
+        fill((dens.at[s, low4], dens_ring.at[s, low4]), 1.0)
 
     @pl.when(b == n_x - 1)
     def _():
-        fill((wide.at[16:], corner.at[4:], ahead.at[:, 12:], back.at[:, 12:], speed.at[:, 12:]), 0.0)
-        fill((dens.at[:, 16:], dens_ring.at[:, 12:]), 1.0)
+        fill((wide.at[16:], corner.at[4:], ahead.at[:, 12:], back.at[:, 12:]), 0.0)
+        fill((speed.at[s, pl.ds(12, 4)],), 0.0)
+        fill((dens.at[:, 16:20],), 1.0)
+        fill((dens.at[s, pl.ds(20, 4)], dens_ring.at[s, pl.ds(12, 4)]), 1.0)
 
     @pl.when(j == 0)
     def _():
-        fill((below, corner.at[:, 4:], ahead_y.at[:, :, 4:], back_y.at[:, :, 4:], speed_y.at[:, :, 4:]), 0.0)
-        fill((dens_far.at[:, :, :4], dens_ring.at[:, :, 4:]), 1.0)
+        fill((below, corner.at[:, 4:], ahead_y.at[:, :, 4:], back_y.at[:, :, 4:]), 0.0)
+        fill((speed_y.at[s, :, high4],), 0.0)
+        fill((dens_ring.at[:, 4:12, 4:],), 1.0)
+        fill((dens_far.at[s, :, low4], dens_ring.at[s, :, high4]), 1.0)
 
     @pl.when(j == n_y - 1)
     def _():
-        fill((above, corner.at[:, :4], ahead_y.at[:, :, :4], back_y.at[:, :, :4], speed_y.at[:, :, :4]), 0.0)
-        fill((dens_far.at[:, :, 4:], dens_ring.at[:, :, :4]), 1.0)
+        fill((above, corner.at[:, :4], ahead_y.at[:, :, :4], back_y.at[:, :, :4]), 0.0)
+        fill((speed_y.at[s, :, low4],), 0.0)
+        fill((dens_ring.at[:, 4:12, :4],), 1.0)
+        fill((dens_far.at[s, :, high4], dens_ring.at[s, :, low4]), 1.0)
 
     pl.semaphore_wait(barrier, n_x - 1 + len(near))
 
@@ -246,26 +257,25 @@
         )
     ]
 
+    ring_s = dens_ring.at[s]
     model = [
         (0, 0, other, density, dens.at[s, pl.ds(8, 8)]),
         (0, 0, other, velocity, speed.at[s, pl.ds(4, 8)]),
     ]
-    outer_model = []
-    for shot in (s, other):
-        ring_s = dens_ring.at[s]
+    for shot in (None, other):
         model += shallow(density, 0, dens.at[s, pl.ds(4, 16)], ring_s.at[pl.ds(4, 8)], shot)
-        outer_model += shallow(velocity, 0, speed.at[s], speed_y.at[s], shot)
-        outer_model += [
-            (1, 0, shot, density.at[first], dens.at[s, pl.ds(0, 4)]),
-            (-1, 0, shot, density.at[final], dens.at[s, pl.ds(20, 4)]),
-            (0, 1, shot, density.at[:, first], dens_far.at[s, :, first]),
-            (0, -1, shot, density.at[:, final], dens_far.at[s, :, final]),
-        ]
-        for dx, dy in diagonals:
-            rows = final if dy > 0 else first
-            here, there = (final, first) if dx > 0 else (first, pl.ds(12, 4))
-            outer_model.append((dx, dy, shot, density.at[here, rows], ring_s.at[there, rows]))
     model = Group(model, model_send, model_recv)
+    outer_model = shallow(velocity, 0, speed.at[s], speed_y.at[s])
+    outer_model += [
+        (1, 0, None, density.at[first], dens.at[s, pl.ds(0, 4)]),
+        (-1, 0, None, density.at[final], dens.at[s, pl.ds(20, 4)]),
+        (0, 1, None, density.at[:, first], dens_far.at[s, :, first]),
+        (0, -1, None, density.at[:, final], dens_far.at[s, :, final]),
+    ]
+    for dx, dy in diagonals:
+        rows = final if dy > 0 else first
+        here, there = (final, first) if dx > 0 else (first, pl.ds(12, 4))
+        outer_model.append((dx, dy, None, density.at[here, rows], ring_s.at[there, rows]))
     groups = [model]
 
     row = lax.broadcasted_iota(jnp.int32, (1, 8, 128), 1)
@@ -402,6 +412,9 @@
         groups.append(group)
         return group
 
+    outer_model = Group(outer_model, outer_send, outer_recv)
+    groups.append(outer_model)
+
     own_model[2].wait()
     arrived = pieces.at[pl.ds(0, n_x - 1)]
     pltpu.make_async_copy(arrived, arrived, piece_sem).wait()
@@ -449,25 +462,37 @@
         copy.wait()
     back_step(0)
 
-    outer_model = Group(outer_model, outer_send, outer_recv)
-    groups.append(outer_model)
-
     exchange.received()
     inner_step(ahead.at[0], ahead_y.at[0], plane_of(old, 0), into(ahead.at[1], 4))
     exchange = send_ahead(1)
+    outer_model.received()
+    for planes in (pl.ds(0, 4), pl.ds(20, 4)):
+        dens[s, planes] = jnp.log(dens[s, planes])
+    for planes in (pl.ds(0, 4), pl.ds(12, 4)):
+        dens_ring[s, planes] = jnp.log(dens_ring[s, planes])
+    dens_far[s] = jnp.log(dens_far[s])
+    handed = [
+        ref.at[s, pl.ds(start, count)]
+        for ref, start, count in (
+            (speed, 0, 4),
+            (speed, 12, 4),
+            (speed_y, 0, 8),
+            (dens, 0, 4),
+            (dens, 20, 4),
+            (dens_ring, 0, 4),
+            (dens_ring, 12, 4),
+            (dens_far, 0, 8),
+        )
+    ]
+    handed = Group([(0, 0, other, ref, ref) for ref in handed], hand_send, hand_recv)
+    groups.append(handed)
     back_step(1)
     exchange.received()
     inner_step(ahead.at[1], ahead_y.at[1], plane_of(ahead.at[0], 4), into(wide, 8))
     exchange = Group(deep(wide, 8, wide, below, above, corner), deep_send, deep_recv)
     groups.append(exchange)
 
-    outer_model.received()
-    for half in range(2):
-        for planes in (slice(0, 4), slice(20, 24)):
-            dens[half, planes] = jnp.log(dens[half, planes])
-        for planes in (slice(0, 4), slice(12, 16)):
-            dens_ring[half, planes] = jnp.log(dens_ring[half, planes])
-        dens_far[half] = jnp.log(dens_far[half])
+    handed.received()
 
     def both(ref, half, low, high):
         return jnp.concatenate([ref[half, low : low + 4], ref[half, high : high + 4]], axis=0)
@@ -637,8 +662,10 @@
             pltpu.SemaphoreType.DMA,
             pltpu.SemaphoreType.DMA((10,)),
             pltpu.SemaphoreType.DMA((10,)),
-            pltpu.SemaphoreType.DMA((24,)),
-            pltpu.SemaphoreType.DMA((24,)),
+            pltpu.SemaphoreType.DMA((12,)),
+            pltpu.SemaphoreType.DMA((12,)),
+            pltpu.SemaphoreType.DMA((8,)),
+            pltpu.SemaphoreType.DMA((8,)),
             pltpu.SemaphoreType.DMA((8,)),
             pltpu.SemaphoreType.DMA((8,)),
             pltpu.SemaphoreType.DMA((2, 4)),

time: 41.4 us -> 39.6 us (0.957)
  Pallas kernels: 40.7 us -> 38.9 us
    pallas_call x1, Pallas kernels: 39.9 us -> 38.1 us  [shards(): pl.pallas_call(functools.partial(kernel, n_x, n_y), out_shape=(pltpu.VMEM...]
where the time goes in v5:
time: 39.6 us; the launch traced here: 39.5 us
  Pallas kernels  38.9 us (98%)
  between operations  0.64 us (2%)
    pallas_call x1, Pallas kernels, shards(): pl.pallas_call(functools.partial(kernel, n_x, n_y), out_shape=(pltpu.VMEM...  38.1 us

profile of v5, /device:TPU:10, one launch (start us, length us, event | category | flops | bytes accessed | tf_op | source)
XLA Modules:
  0.0 39.5 jit_solution(10437353162613489213)
XLA Ops:
  0.6 38.1 %shard_map.94 = (f32[8,8,128]{2,1,0:T(8,128)S(1)}, f32[1,2,8,8,256]{4,3,2,1,0:T(8,128)S(1)}, f32[1,2,8,8,256]{4,3,2,1,0:T(8,128)S(1)}) custom-call(f32[8,8,128]{2,1,0:T(8,128)} %velocity.1, f32[8,8,128]{2,1,0:T(8,128)} %density.1, f32[32,2,2,256]{3,2,1,0:T(2,128)} %stored.1, s32[1,32]{1,0:T(1,128)} %holders.1, f32[1,2,8,8,256]{4,3,2,1,0:T(8,128)} %adjoint.1, ...), custom_call_target="tpu_custom_call" | custom-call | flops 8000000 | bytes 800000 | tf_op jit(solution)/shard_map/pallas_call | solution.py:620
  38.8 0.7 %shard_map.95 = (f32[8,8,128]{2,1,0:T(8,128)}, f32[1,2,8,8,256]{4,3,2,1,0:T(8,128)}, f32[1,2,8,8,256]{4,3,2,1,0:T(8,128)}) custom-call(f32[8,8,128]{2,1,0:T(8,128)S(1)} %get-tuple-element.6.image, f32[1,2,8,8,256]{4,3,2,1,0:T(8,128)S(1)} %get-tuple-element.7.forward, f32[1,2,8,8,256]{4,3,2,1,0:T(8,128)S(1)} %get-tuple-element.8.adjoint), custom_call_target="tpu_custom_call" | custom-call | tf_op jit(solution)/shard_map/pallas_call | solution.py:686

commit v6 on v5

--- a/solution.py
+++ b/solution.py
@@ -68,6 +68,7 @@
     back_y,
     back_old,
     last,
+    part,
     coef,
     coef_y,
     dens,
@@ -251,20 +252,20 @@
         entries.append((0, -1, shot, whole, upper))
         return entries
 
+    ring_s = dens_ring.at[s]
+    model = [
+        (0, 0, other, density, dens.at[s, pl.ds(8, 8)]),
+        (0, 0, other, velocity, speed.at[s, pl.ds(4, 8)]),
+    ]
+    for shot in (None, other):
+        model += shallow(density, 0, dens.at[s, pl.ds(4, 16)], ring_s.at[pl.ds(4, 8)], shot)
+    model = Group(model, model_send, model_recv)
     backs = [
         Group(
             shallow(adjoint.at[0, 0], 0, back.at[0], back_y.at[0]), back_send.at[0], back_recv.at[0]
         )
     ]
 
-    ring_s = dens_ring.at[s]
-    model = [
-        (0, 0, other, density, dens.at[s, pl.ds(8, 8)]),
-        (0, 0, other, velocity, speed.at[s, pl.ds(4, 8)]),
-    ]
-    for shot in (None, other):
-        model += shallow(density, 0, dens.at[s, pl.ds(4, 16)], ring_s.at[pl.ds(4, 8)], shot)
-    model = Group(model, model_send, model_recv)
     outer_model = shallow(velocity, 0, speed.at[s], speed_y.at[s])
     outer_model += [
         (1, 0, None, density.at[first], dens.at[s, pl.ds(0, 4)]),
@@ -382,6 +383,60 @@
             put,
         )
 
+    def begin_step(planes, base, before):
+        own = plane_of(planes, base)
+
+        def one(p, carry):
+            centre = [own(p, lanes) for lanes in halves]
+            place = pl.ds(4 + p, 1)
+            total = [
+                coef[0, place, :, lanes] * centre[half] - before(p, lanes)
+                for half, lanes in enumerate(halves)
+            ]
+            for k in range(1, 5):
+                at = 1 + 6 * (k - 1)
+                up = z_plus(centre[0], centre[1], lane, k)
+                down = z_minus(centre[0], centre[1], lane, k)
+                for half, lanes in enumerate(halves):
+                    plus = jnp.where(row < 8 - k, pltpu.roll(centre[half], 8 - k, 1), 0.0)
+                    minus = jnp.where(row >= k, pltpu.roll(centre[half], k, 1), 0.0)
+                    total[half] = (
+                        total[half]
+                        + coef[at + 2, place, :, lanes] * plus
+                        + coef[at + 3, place, :, lanes] * minus
+                        + coef[at + 4, place, :, lanes] * up[half]
+                        + coef[at + 5, place, :, lanes] * down[half]
+                    )
+            for half, lanes in enumerate(halves):
+                part[pl.ds(p, 1), :, lanes] = total[half]
+            return carry
+
+        lax.fori_loop(0, 8, one, 0, unroll=True)
+
+    def end_step(planes, base, edge, put):
+        own = plane_of(planes, base)
+
+        def one(p, carry):
+            place = pl.ds(4 + p, 1)
+            for half, lanes in enumerate(halves):
+                total = part[pl.ds(p, 1), :, lanes]
+                around = edge(p, lanes)
+                for k in range(1, 5):
+                    at = 1 + 6 * (k - 1)
+                    plus = jnp.where(row >= 8 - k, pltpu.roll(around, 8 - k, 1), 0.0)
+                    minus = jnp.where(row < k, pltpu.roll(around, k, 1), 0.0)
+                    total = (
+                        total
+                        + coef[at, place, :, lanes] * own(p, lanes, k)
+                        + coef[at + 1, place, :, lanes] * own(p, lanes, -k)
+                        + coef[at + 2, place, :, lanes] * plus
+                        + coef[at + 3, place, :, lanes] * minus
+                    )
+                put(p, lanes, total, half)
+            return carry
+
+        lax.fori_loop(0, 8, one, 0, unroll=True)
+
     def back_step(level):
         backs[level].received()
         before = plane_of(back_old, 0) if level == 0 else plane_of(back.at[level - 1], 4)
@@ -462,8 +517,9 @@
         copy.wait()
     back_step(0)
 
+    begin_step(ahead.at[0], 4, plane_of(old, 0))
     exchange.received()
-    inner_step(ahead.at[0], ahead_y.at[0], plane_of(old, 0), into(ahead.at[1], 4))
+    end_step(ahead.at[0], 4, plane_of(ahead_y.at[0], 0), into(ahead.at[1], 4))
     exchange = send_ahead(1)
     outer_model.received()
     for planes in (pl.ds(0, 4), pl.ds(20, 4)):
@@ -487,11 +543,13 @@
     handed = Group([(0, 0, other, ref, ref) for ref in handed], hand_send, hand_recv)
     groups.append(handed)
     back_step(1)
+    begin_step(ahead.at[1], 4, plane_of(ahead.at[0], 4))
     exchange.received()
-    inner_step(ahead.at[1], ahead_y.at[1], plane_of(ahead.at[0], 4), into(wide, 8))
+    end_step(ahead.at[1], 4, plane_of(ahead_y.at[1], 0), into(wide, 8))
     exchange = Group(deep(wide, 8, wide, below, above, corner), deep_send, deep_recv)
     groups.append(exchange)
 
+    back_step(2)
     handed.received()
 
     def both(ref, half, low, high):
@@ -522,7 +580,6 @@
         lambda half, k: y_minus_outer(dens[half, 8:16], dens_above[half], dens_below[half], row, k),
     )
 
-    back_step(2)
     outs = [pltpu.make_async_copy(back.at[3, pl.ds(4, 8)], adjoint_out.at[0, 1], out_sem.at[0])]
     outs[0].start()
     early = [
@@ -531,6 +588,7 @@
         for lanes in halves
     ]
 
+    begin_step(wide, 8, plane_of(ahead.at[1], 4))
     exchange.received()
     for lanes in halves:
         ring[0:4, :, lanes] = corner[0:4, :, lanes]
@@ -552,18 +610,20 @@
         plane_of(ahead_y.at[1], 0),
         into(mid_y, 0),
     )
-    around = plane_of(ring, 0)
-    steps(
-        16,
-        coef,
-        0,
-        plane_of(wide, 4),
-        plane_of(wide, 4),
-        lambda p, lanes, centre, k: y_plus(centre, around(p, lanes), row, k),
-        lambda p, lanes, centre, k: y_minus(centre, around(p, lanes), row, k),
-        plane_of(ahead.at[1], 0),
-        into(mid, 0),
-    )
+    for start in (0, 12):
+        around = plane_of(ring, start)
+        steps(
+            4,
+            coef,
+            start,
+            plane_of(wide, 4 + start),
+            plane_of(wide, 4 + start),
+            lambda p, lanes, centre, k: y_plus(centre, around(p, lanes), row, k),
+            lambda p, lanes, centre, k: y_minus(centre, around(p, lanes), row, k),
+            plane_of(ahead.at[1], start),
+            into(mid, start),
+        )
+    end_step(wide, 8, plane_of(ring, 4), into(mid, 4))
     outs.append(pltpu.make_async_copy(mid.at[pl.ds(4, 8)], forward_out.at[0, 1], out_sem.at[1]))
     outs[1].start()
     inner_step(mid, mid_y, plane_of(wide, 8), into(last.at[0], 0))
@@ -641,6 +701,7 @@
             pltpu.VMEM((STEPS, 8, 8, 256), f32),
             pltpu.VMEM((8, 8, 256), f32),
             pltpu.VMEM((2, 8, 8, 256), f32),
+            pltpu.VMEM((8, 8, 256), f32),
             pltpu.VMEM((25, 16, 8, 256), f32),
             pltpu.VMEM((25, 8, 8, 256), f32),
             pltpu.VMEM((2, 24, 8, 128), f32),

time: 39.6 us -> 38.7 us (0.977)
  the two profiles are of different devices: /device:TPU:10 before, /device:TPU:1 now
where the time goes in v6:
time: 38.7 us; the launch traced here: 38.6 us
  Pallas kernels  38 us (98%)
  between operations  0.64 us (2%)
    pallas_call x1, Pallas kernels, shards(): pl.pallas_call(functools.partial(kernel, n_x, n_y), out_shape=(pltpu.VMEM...  37.2 us

profile of v6, /device:TPU:1, one launch (start us, length us, event | category | flops | bytes accessed | tf_op | source)
XLA Modules:
  0.0 38.6 jit_solution(7631773550947541543)
XLA Ops:
  0.6 37.2 %shard_map.94 = (f32[8,8,128]{2,1,0:T(8,128)S(1)}, f32[1,2,8,8,256]{4,3,2,1,0:T(8,128)S(1)}, f32[1,2,8,8,256]{4,3,2,1,0:T(8,128)S(1)}) custom-call(f32[8,8,128]{2,1,0:T(8,128)} %velocity.1, f32[8,8,128]{2,1,0:T(8,128)} %density.1, f32[32,2,2,256]{3,2,1,0:T(2,128)} %stored.1, s32[1,32]{1,0:T(1,128)} %holders.1, f32[1,2,8,8,256]{4,3,2,1,0:T(8,128)} %adjoint.1, ...), custom_call_target="tpu_custom_call" | custom-call | flops 8000000 | bytes 800000 | tf_op jit(solution)/shard_map/pallas_call | solution.py:680
  37.9 0.7 %shard_map.95 = (f32[8,8,128]{2,1,0:T(8,128)}, f32[1,2,8,8,256]{4,3,2,1,0:T(8,128)}, f32[1,2,8,8,256]{4,3,2,1,0:T(8,128)}) custom-call(f32[8,8,128]{2,1,0:T(8,128)S(1)} %get-tuple-element.6.image, f32[1,2,8,8,256]{4,3,2,1,0:T(8,128)S(1)} %get-tuple-element.7.forward, f32[1,2,8,8,256]{4,3,2,1,0:T(8,128)S(1)} %get-tuple-element.8.adjoint), custom_call_target="tpu_custom_call" | custom-call | tf_op jit(solution)/shard_map/pallas_call | solution.py:747

commit v7 on v6

--- a/solution.py
+++ b/solution.py
@@ -626,24 +626,44 @@
     end_step(wide, 8, plane_of(ring, 4), into(mid, 4))
     outs.append(pltpu.make_async_copy(mid.at[pl.ds(4, 8)], forward_out.at[0, 1], out_sem.at[1]))
     outs[1].start()
-    inner_step(mid, mid_y, plane_of(wide, 8), into(last.at[0], 0))
-    whole = [
-        active
-        * (
-            early[half]
-            + mid[4:12, :, lanes] * back[1, 4:12, :, lanes]
-            + last[0, :, :, lanes] * back[0, 4:12, :, lanes]
+    to_partner = []
+    for start in (0, 4):
+        edge = plane_of(mid_y, start)
+        steps(
+            4,
+            coef,
+            4 + start,
+            plane_of(mid, 4 + start),
+            plane_of(mid, 4 + start),
+            lambda p, lanes, centre, k: y_plus(centre, edge(p, lanes), row, k),
+            lambda p, lanes, centre, k: y_minus(centre, edge(p, lanes), row, k),
+            plane_of(wide, 8 + start),
+            into(last.at[0], start),
         )
-        for half, lanes in enumerate(halves)
-    ]
-    share[...] = jnp.where(s == 0, whole[1], whole[0])
-    to_partner = pltpu.make_async_remote_copy(
-        share, partner_share, image_sem.at[0], image_sem.at[1], device_id={"shot": other}
-    )
-    to_partner.start()
+        some = pl.ds(start, 4)
+        inner = pl.ds(4 + start, 4)
+        whole = [
+            active
+            * (
+                early[half][start : start + 4]
+                + mid[inner, :, lanes] * back[1, inner, :, lanes]
+                + last[0, some, :, lanes] * back[0, inner, :, lanes]
+            )
+            for half, lanes in enumerate(halves)
+        ]
+        share[some] = jnp.where(s == 0, whole[1], whole[0])
+        copy = pltpu.make_async_remote_copy(
+            share.at[some],
+            partner_share.at[some],
+            image_sem.at[0, start // 4],
+            image_sem.at[1, start // 4],
+            device_id={"shot": other},
+        )
+        copy.start()
+        to_partner.append(copy)
+        image_out[some] = jnp.where(s == 0, whole[0], whole[1])
     outs.append(pltpu.make_async_copy(last.at[0], forward_out.at[0, 0], out_sem.at[2]))
     outs[2].start()
-    image_out[...] = jnp.where(s == 0, whole[0], whole[1])
 
     back_step(3)
     outs.append(pltpu.make_async_copy(last.at[1], adjoint_out.at[0, 0], out_sem.at[3]))
@@ -654,7 +674,8 @@
     for group in groups + backs:
         group.sent()
 
-    to_partner.wait()
+    for copy in to_partner:
+        copy.wait()
     image_out[...] += partner_share[...]
     for copy in outs:
         copy.wait()
@@ -733,7 +754,7 @@
             pltpu.SemaphoreType.DMA((2, 4)),
             pltpu.SemaphoreType.DMA((STEPS, 4)),
             pltpu.SemaphoreType.DMA((STEPS, 4)),
-            pltpu.SemaphoreType.DMA((2,)),
+            pltpu.SemaphoreType.DMA((2, 2)),
             pltpu.SemaphoreType.DMA((4,)),
         ],
         compiler_params=pltpu.CompilerParams(

time: 38.7 us -> 38.6 us (level)
  no operation moved by 1% of the time
where the time goes in v7:
time: 38.6 us; the launch traced here: 38.5 us
  Pallas kernels  37.9 us (98%)
  between operations  0.64 us (2%)
    pallas_call x1, Pallas kernels, shards(): pl.pallas_call(functools.partial(kernel, n_x, n_y), out_shape=(pltpu.VMEM...  37.2 us

profile of v7, /device:TPU:1, one launch (start us, length us, event | category | flops | bytes accessed | tf_op | source)
XLA Modules:
  0.0 38.5 jit_solution(2919200016434939310)
XLA Ops:
  0.6 37.2 %shard_map.94 = (f32[8,8,128]{2,1,0:T(8,128)S(1)}, f32[1,2,8,8,256]{4,3,2,1,0:T(8,128)S(1)}, f32[1,2,8,8,256]{4,3,2,1,0:T(8,128)S(1)}) custom-call(f32[8,8,128]{2,1,0:T(8,128)} %velocity.1, f32[8,8,128]{2,1,0:T(8,128)} %density.1, f32[32,2,2,256]{3,2,1,0:T(2,128)} %stored.1, s32[1,32]{1,0:T(1,128)} %holders.1, f32[1,2,8,8,256]{4,3,2,1,0:T(8,128)} %adjoint.1, ...), custom_call_target="tpu_custom_call" | custom-call | flops 8000000 | bytes 800000 | tf_op jit(solution)/shard_map/pallas_call | solution.py:701
  37.8 0.7 %shard_map.95 = (f32[8,8,128]{2,1,0:T(8,128)}, f32[1,2,8,8,256]{4,3,2,1,0:T(8,128)}, f32[1,2,8,8,256]{4,3,2,1,0:T(8,128)}) custom-call(f32[8,8,128]{2,1,0:T(8,128)S(1)} %get-tuple-element.6.image, f32[1,2,8,8,256]{4,3,2,1,0:T(8,128)S(1)} %get-tuple-element.7.forward, f32[1,2,8,8,256]{4,3,2,1,0:T(8,128)S(1)} %get-tuple-element.8.adjoint), custom_call_target="tpu_custom_call" | custom-call | tf_op jit(solution)/shard_map/pallas_call | solution.py:768
